TPU v7x, 32 devices: a whole 2x2x4 slice. The times are simulated.
32 devices in a mesh: group: 2 (over y), member: 4 (over z), tile: 2 (over x), sample: 2 (over core).
Axes of the slice: x: 2, y: 2, z: 4, core: 2. Of those that a mesh axis runs over, the one named last changes fastest.
Arguments:
- latent: bfloat16 [4, 4, 4, 512, 256], P(('group', 'sample'), 'member', None, 'tile'), parts along dimension 0, may hold values from -6 to 6
- observed: float32 [4, 8, 4, 512], P(('group', 'sample'), None, None, 'tile'), parts along dimension 0, may hold values from -6 to 6
- radar_valid: int32 [4, 4, 512], P(('group', 'sample'), None, 'tile'), parts along dimension 0, may hold values 0 or 1
- member_order: int32 [4, 4], P(('group', 'sample'), 'member'), parts along dimension 0, may hold values from 0 to 3, each once within a row
- weight_in: bfloat16 [256, 128], replicated, may hold values from -0.375 to 0.375
- weight_mid: bfloat16 [128, 128], replicated, may hold values from -0.5 to 0.5
- weight_out: bfloat16 [128, 8], replicated, may hold values from -0.5 to 0.5
- gains: float32 [4, 128], replicated, may hold values from 0.1 to 1.9
Outputs:
- pixel_score: float32 [4, 8, 4, 512], P(('group', 'sample'), None, 'member', 'tile'), parts along dimension 0
- grad_in: float32 [512, 128], P('group'), parts along dimension 0
- grad_mid: float32 [256, 128], P('group'), parts along dimension 0
- grad_out: float32 [256, 8], P('group'), parts along dimension 0
- grad_gains: float32 [8, 128], P('group'), parts along dimension 0
There are 2 independent parts, one for each index of `group`. A program takes and returns all parts, laid end to end along the dimension named above; an argument that names none is the same for every part. Nothing has to cross between parts.
Inputs may be any that keep to these rules, and one draw needn't show every extreme that they name: `member_order`: for each sample, each member number appears in exactly one slot.
All inputs are finite; a program needn't handle non-finite values. No bound on the sum of `radar_valid` on one device may be relied on, other than what follows from the above.
Results may differ from a plain program's by a relative error of at most 0.0046.
Values may be sent and summed in bfloat16 or wider, within the bound.
No kernel may reach another device: no remote copies, remote signals or barrier semaphores. Data moves between devices by JAX's collectives and lax.ppermute only.
A program may use at most 64 MiB of HBM per device.

v0:
```python
import math

import jax
import jax.numpy as jnp
from jax import lax
from jax.sharding import PartitionSpec as P

gelu_coef = 0.7978845608028654
cubic_coef = 0.044715
soft_square = 0.0625


def gelu_pair(values):
    inner = jnp.tanh(gelu_coef * (values + cubic_coef * values * values * values))
    output = 0.5 * values * (1.0 + inner)
    slope_part = 0.5 * (1.0 + inner) + 0.5 * values * (1.0 - inner * inner) * gelu_coef * (
        1.0 + 3.0 * cubic_coef * values * values
    )
    return (output, slope_part)


def soft_pair(values):
    magnitude = jnp.sqrt(values * values + soft_square)
    return (magnitude, values / magnitude)


def on_device(
    latent, observed, radar_valid, member_order, weight_in, weight_mid, weight_out, gains
):
    row_count = latent.shape[2]
    tile_cols = latent.shape[3]
    width = latent.shape[4]
    fields = weight_out.shape[1]
    members = lax.axis_size("member")
    col_count = tile_cols * lax.axis_size("tile")
    norm_factor = 1.0 / math.sqrt(lax.axis_size("sample") * row_count * col_count)
    pair_norm = 2.0 * members * (members - 1)
    selector = (jnp.arange(members, dtype=jnp.int32) == member_order[0, 0]).astype(jnp.float32)
    gain_row = jnp.sum(selector[:, None] * gains, axis=0)
    inputs = latent[0, 0].reshape(row_count * tile_cols, width)
    pre_one = jnp.dot(inputs, weight_in, preferred_element_type=jnp.float32)
    act_one, slope_one = gelu_pair(pre_one)
    hidden_one = (act_one * gain_row).astype(jnp.bfloat16)
    pre_two = jnp.dot(hidden_one, weight_mid, preferred_element_type=jnp.float32)
    act_two, slope_two = gelu_pair(pre_two)
    hidden_two = act_two.astype(jnp.bfloat16)
    predicted = lax.dot_general(
        weight_out, hidden_two, (((0,), (1,)), ((), ())), preferred_element_type=jnp.float32
    )
    predicted = predicted.reshape(1, fields, row_count, tile_cols)
    mine = predicted[0]
    magnitude, slope = soft_pair(
        mine[None] - lax.all_gather(predicted, "member", axis=0, tiled=True)
    )
    spread = jnp.sum(magnitude, axis=0)
    slopes = jnp.sum(slope, axis=0)
    target = observed[0]
    is_valid = radar_valid[0].astype(jnp.float32)[None]
    own_mag, own_slope = soft_pair(mine - target)
    term = is_valid * (own_mag / members - spread / pair_norm)
    pixel_score = lax.psum_scatter(term[None], "member", scatter_dimension=2, tiled=True)
    grad_pred = (
        norm_factor * is_valid * (own_slope / members - slopes / (members * (members - 1.0)))
    )
    grad_pred = grad_pred.astype(jnp.bfloat16)
    grad_flat = grad_pred.reshape(fields, row_count * tile_cols)
    grad_out = lax.dot_general(
        hidden_two, grad_flat, (((0,), (1,)), ((), ())), preferred_element_type=jnp.float32
    )
    grad_hid_two = lax.dot_general(
        grad_flat, weight_out, (((0,), (1,)), ((), ())), preferred_element_type=jnp.float32
    )
    grad_pre_two = (grad_hid_two * slope_two).astype(jnp.bfloat16)
    grad_mid = lax.dot_general(
        hidden_one, grad_pre_two, (((0,), (0,)), ((), ())), preferred_element_type=jnp.float32
    )
    grad_hid_one = lax.dot_general(
        grad_pre_two, weight_mid, (((1,), (1,)), ((), ())), preferred_element_type=jnp.float32
    )
    grad_gain_row = jnp.sum(grad_hid_one * act_one, axis=0)
    grad_pre_one = (grad_hid_one * gain_row * slope_one).astype(jnp.bfloat16)
    grad_in = lax.dot_general(
        inputs, grad_pre_one, (((0,), (0,)), ((), ())), preferred_element_type=jnp.float32
    )
    grad_gains = selector[:, None] * grad_gain_row[None, :]
    grad_in, grad_mid, grad_out, grad_gains = lax.psum(
        (grad_in, grad_mid, grad_out, grad_gains), ("member", "tile", "sample")
    )
    return (pixel_score, grad_in, grad_mid, grad_out, grad_gains)


def solution(mesh):
    placed = (
        P(("group", "sample"), "member", None, "tile", None),
        P(("group", "sample"), None, None, "tile"),
        P(("group", "sample"), None, "tile"),
        P(("group", "sample"), "member"),
        P(),
        P(),
        P(),
        P(),
    )
    return jax.shard_map(
        on_device,
        mesh=mesh,
        in_specs=placed,
        out_specs=(
            P(("group", "sample"), None, "member", "tile"),
            P("group", None),
            P("group", None),
            P("group", None),
            P("group", None),
        ),
        check_vma=False,
    )
```

profile of v0, /device:TPU:0, one launch (start us, length us, event | category | flops | bytes accessed | tf_op | source)
XLA Modules:
  0.0 134.0 jit_solution(13403448466728375083)
XLA Ops:
  8.0 0.0 copy-start
  8.0 0.0 reduce-scatter.2.cloned.1.call-start
  8.8 0.0 copy-start.5
  8.8 0.7 copy-done.5
  9.4 0.1 multiply_reduce_fusion.1
  9.5 0.0 copy-done
  9.5 1.2 multiply_convert_fusion.1
  10.7 0.0 copy-done.6
  10.7 0.0 copy-start.4
  10.8 0.3 multiply_convert_fusion
  11.1 0.3 copy-done.4
  11.4 0.2 fusion.27
  11.6 15.2 %all_gather.3 = f32[4,8,4,256]{3,1,2,0:T(8,128)S(1)} all-gather(f32[1,8,4,256]{3,1,2,0:T(8,128)S(1)} %bitcast.47), channel_id=1, replica_groups=mesh['group'=2,'member'=4,'tile'=2,'sample'=2] {'member'}, dimensions={0}, use_global_device_ids=true | all-gather | bytes 163840 | tf_op jit(solution)/shard_map/all_gather | solution.py:53
  26.8 0.0 copy-done.3
  26.8 0.1 divide_reduce_fusion
  26.9 0.7 copy-done.2
  27.6 0.6 fusion.26
  28.2 0.0 reduce-scatter.2.cloned.1.call-update
  28.2 0.0 all-reduce.4.cloned.1.call-start
  28.3 0.5 fusion
  28.8 0.3 multiply_reduce_fusion
  29.1 1.2 convolution_bitcast_fusion
  30.4 0.9 fusion.28
  31.3 0.0 all-reduce.4.cloned.1.call-update
  31.3 0.1 fusion.29
  31.4 0.1 broadcast_multiply_fusion.1
  31.5 31.5 %all-reduce = (f32[128,8]{0,1:T(8,128)}, f32[4,128]{1,0:T(4,128)}) all-reduce(f32[128,8]{0,1:T(8,128)S(1)} %fusion.29, f32[4,128]{1,0:T(4,128)S(1)} %broadcast_multiply_fusion.1), channel_id=1, replica_groups=mesh['group'=2,'member'=4,'tile'=2,'sample'=2] {'member','tile','sample'}, use_global_device_ids=true, to_apply=%region_6.0 | all-reduce | flops 1536 | bytes 12288 | tf_op jit(solution)/shard_map/psum | solution.py:86
  63.0 1.3 copy.17
  64.3 60.0 %all-reduce.4.cloned.1.call-done = (f32[256,128]{0,1:T(8,128)}, f32[128,128]{1,0:T(8,128)}) async-done(((f32[256,128]{0,1:T(8,128)}, f32[128,128]{1,0:T(8,128)}), (f32[256,128]{0,1:T(8,128)}, f32[128,128]{1,0:T(8,128)})) %all-reduce.4.cloned.1.call-update) | async-done | bytes 196624 | tf_op jit(solution)/shard_map/psum | solution.py:86
  124.3 1.7 %copy.18 = f32[256,128]{1,0:T(8,128)} copy(f32[256,128]{0,1:T(8,128)} %get-tuple-element.19) | data formatting | bytes 262144
  126.0 0.0 copy-done.1
  126.0 0.6 copy.36
  (11 shorter events, 0.0 us)
Async XLA Ops:
  8.0 1.5 %copy-start = (bf16[1,1,4,256,256]{4,3,2,1,0:T(8,128)(2,1)S(1)}, bf16[1,1,4,256,256]{4,3,2,1,0:T(8,128)(2,1)}, u32[]{:S(2)}) copy-start(bf16[1,1,4,256,256]{4,3,2,1,0:T(8,128)(2,1)} %param.8) | copy-start | bytes 1572868
  8.0 55.0 %reduce-scatter.2.cloned.1.call-start = ((), (), s32[]{:S(2)}) async-start(), calls=%async_computation.1 | async-start | bytes 40960 | tf_op jit(solution)/shard_map/reduce_scatter | solution.py:61
  8.8 0.7 copy-start.5
  9.5 1.2 copy-start.6
  10.7 0.7 copy-start.4
  11.6 15.2 %copy-start.3 = (s32[1,4,256]{2,1,0:T(4,128)S(1)}, s32[1,4,256]{2,1,0:T(4,128)}, u32[]{:S(2)}) copy-start(s32[1,4,256]{2,1,0:T(4,128)} %param.10) | copy-start | bytes 12292
  26.8 0.8 copy-start.2
  28.2 96.0 %all-reduce.4.cloned.1.call-start = ((), (), s32[]{:S(2)}) async-start(), calls=%async_computation.2 | async-start | bytes 393216 | tf_op jit(solution)/shard_map/psum | solution.py:86
  124.3 1.7 %copy-start.1 = (f32[128,128]{1,0:T(8,128)S(1)}, f32[128,128]{1,0:T(8,128)}, u32[]{:S(2)}) copy-start(f32[128,128]{1,0:T(8,128)} %get-tuple-element.31) | copy-start | bytes 196612
Sparse Core Ops, SparseCore 0:
  28.3 20.3 reduce-scatter.1
Sparse Core Ops, SparseCore 1:
  33.2 91.0 all-reduce.3
where the time goes:
time: 134 us
  waiting for transfers between devices  60 us (45%)
  blocking collectives  46.7 us (35%)
  between operations  16.3 us (12%)
  local copies, waits for them, and re-layouts  5.34 us (4%)
  matrix products  4.76 us (4%)
    psum x1, waiting for transfers between devices, on_device(): lax.psum((grad_in, grad_mid, grad_out, grad_gains), ('member', 'tile', 's...  60 us
    psum x1, blocking collectives, on_device(): lax.psum((grad_in, grad_mid, grad_out, grad_gains), ('member', 'tile', 's...  31.5 us
    all_gather x1, blocking collectives, on_device(): lax.all_gather(predicted, 'member', axis=0, tiled=True)  15.2 us
    unnamed x18, local copies, waits for them, and re-layouts  5.34 us
  transfers between devices with their start and end apart: 2, of which 1 were waited for; matrix products, arithmetic and copies ran while one was open for 3% of the time, Pallas kernels for 0%

commit v1 on v0

--- a/solution.py
+++ b/solution.py
@@ -8,6 +8,7 @@
 gelu_coef = 0.7978845608028654
 cubic_coef = 0.044715
 soft_square = 0.0625
+mesh_axes = ("member", "tile", "sample")
 
 
 def gelu_pair(values):
@@ -24,6 +25,60 @@
     return (magnitude, values / magnitude)
 
 
+def swap(array, offset):
+    count = 1
+    for axis in mesh_axes:
+        count *= lax.axis_size(axis)
+    return lax.ppermute(array, mesh_axes, [(place, place ^ offset) for place in range(count)])
+
+
+def rounds_of(bits):
+    return [bits[first : first + 2] for first in range(0, len(bits), 2)]
+
+
+def bits_of(size, lowest):
+    assert size & (size - 1) == 0
+    return [lowest << place for place in range(size.bit_length() - 1)]
+
+
+def gather_members(block):
+    unit = lax.axis_size("tile") * lax.axis_size("sample")
+    stack = [block]
+    for bits in rounds_of(bits_of(lax.axis_size("member"), unit)):
+        whole = jnp.stack(stack)
+        offsets = bits if len(bits) == 1 else [bits[0], bits[1], bits[0] ^ bits[1]]
+        arrived = [swap(whole, offset) for offset in offsets]
+        stack = stack + [part[k] for part in arrived for k in range(len(stack))]
+    return stack
+
+
+def sum_parameters(rows, link_dtype):
+    half = rows.shape[0] // 2
+    tiles, samples = lax.axis_size("tile"), lax.axis_size("sample")
+    bits = bits_of(tiles, samples) + bits_of(lax.axis_size("member"), samples * tiles)
+    place = lax.axis_index(mesh_axes)
+    which = place & 1
+    for bit in bits:
+        which = which ^ jnp.where(place & bit, 1, 0)
+    keep = lax.dynamic_slice_in_dim(rows, which * half, half)
+    away = lax.dynamic_slice_in_dim(rows, (1 - which) * half, half)
+    total = keep + swap(away, 1)
+    for group in rounds_of(bits):
+        sent = total.astype(link_dtype)
+        if len(group) == 1:
+            arrived = swap(sent, group[0] ^ 1)
+            total = sent.astype(jnp.float32) + arrived.astype(jnp.float32)
+        else:
+            near, far = group
+            parts = [swap(sent, near ^ 1), swap(sent, far ^ 1), swap(sent, near ^ far)]
+            parts = [part.astype(jnp.float32) for part in parts]
+            total = (sent.astype(jnp.float32) + parts[0]) + (parts[1] + parts[2])
+    other = swap(total, 1)
+    first = jnp.where(which == 0, total, other)
+    second = jnp.where(which == 0, other, total)
+    return jnp.concatenate([first, second], axis=0)
+
+
 def on_device(
     latent, observed, radar_valid, member_order, weight_in, weight_mid, weight_out, gains
 ):
@@ -31,6 +86,7 @@
     tile_cols = latent.shape[3]
     width = latent.shape[4]
     fields = weight_out.shape[1]
+    hidden = weight_mid.shape[0]
     members = lax.axis_size("member")
     col_count = tile_cols * lax.axis_size("tile")
     norm_factor = 1.0 / math.sqrt(lax.axis_size("sample") * row_count * col_count)
@@ -47,25 +103,32 @@
     predicted = lax.dot_general(
         weight_out, hidden_two, (((0,), (1,)), ((), ())), preferred_element_type=jnp.float32
     )
-    predicted = predicted.reshape(1, fields, row_count, tile_cols)
-    mine = predicted[0]
-    magnitude, slope = soft_pair(
-        mine[None] - lax.all_gather(predicted, "member", axis=0, tiled=True)
-    )
-    spread = jnp.sum(magnitude, axis=0)
-    slopes = jnp.sum(slope, axis=0)
+    mine = predicted.reshape(fields, row_count, tile_cols)
+    ensemble = gather_members(mine.astype(jnp.bfloat16))
+    others = jnp.stack([part.astype(jnp.float32) for part in ensemble[1:]])
     target = observed[0]
     is_valid = radar_valid[0].astype(jnp.float32)[None]
-    own_mag, own_slope = soft_pair(mine - target)
-    term = is_valid * (own_mag / members - spread / pair_norm)
-    pixel_score = lax.psum_scatter(term[None], "member", scatter_dimension=2, tiled=True)
+    own_slope = soft_pair(mine - target)[1]
+    slopes = jnp.sum(soft_pair(mine[None] - others)[1], axis=0)
     grad_pred = (
         norm_factor * is_valid * (own_slope / members - slopes / (members * (members - 1.0)))
     )
     grad_pred = grad_pred.astype(jnp.bfloat16)
+
+    own_rows = row_count // members
+    first_row = lax.axis_index("member") * own_rows
+    row_all = lax.dynamic_slice_in_dim(
+        jnp.concatenate([mine[None], others]), first_row, own_rows, axis=2
+    )
+    row_target = lax.dynamic_slice_in_dim(target, first_row, own_rows, axis=1)
+    row_valid = lax.dynamic_slice_in_dim(is_valid, first_row, own_rows, axis=1)
+    skill = jnp.sum(soft_pair(row_all - row_target[None])[0], axis=0)
+    spread = jnp.sum(soft_pair(row_all[:, None] - row_all[None])[0], axis=(0, 1))
+    pixel_score = (row_valid * (skill / members - spread / pair_norm))[None]
+
     grad_flat = grad_pred.reshape(fields, row_count * tile_cols)
     grad_out = lax.dot_general(
-        hidden_two, grad_flat, (((0,), (1,)), ((), ())), preferred_element_type=jnp.float32
+        grad_flat, hidden_two, (((1,), (0,)), ((), ())), preferred_element_type=jnp.float32
     )
     grad_hid_two = lax.dot_general(
         grad_flat, weight_out, (((0,), (1,)), ((), ())), preferred_element_type=jnp.float32
@@ -83,10 +146,21 @@
         inputs, grad_pre_one, (((0,), (0,)), ((), ())), preferred_element_type=jnp.float32
     )
     grad_gains = selector[:, None] * grad_gain_row[None, :]
-    grad_in, grad_mid, grad_out, grad_gains = lax.psum(
-        (grad_in, grad_mid, grad_out, grad_gains), ("member", "tile", "sample")
+
+    used = width + hidden + fields + members
+    padded = -(-used // 32) * 32
+    rows = jnp.concatenate(
+        [grad_in, grad_mid, grad_out, grad_gains, jnp.zeros((padded - used, hidden), jnp.float32)]
     )
-    return (pixel_score, grad_in, grad_mid, grad_out, grad_gains)
+    rows = sum_parameters(rows, jnp.bfloat16)
+    cuts = [width, width + hidden, width + hidden + fields, used]
+    return (
+        pixel_score,
+        rows[: cuts[0]],
+        rows[cuts[0] : cuts[1]],
+        rows[cuts[1] : cuts[2]].T,
+        rows[cuts[2] : cuts[3]],
+    )
 
 
 def solution(mesh):

time: 134 us -> 35.7 us (0.27)
  waiting for transfers between devices: 60 us -> 12.6 us
  blocking collectives: 46.7 us -> 0 us
  between operations: 16.3 us -> 1.6 us
  starting transfers between devices: 0.08 us -> 11.4 us
    psum x1 -> x0, waiting for transfers between devices: 60 us -> none  [on_device(): lax.psum((grad_in, grad_mid, grad_out, grad_gains), ('member', 'tile', 's...]
    psum x1 -> x0, blocking collectives: 31.5 us -> none  [on_device(): lax.psum((grad_in, grad_mid, grad_out, grad_gains), ('member', 'tile', 's...]
    all_gather x1 -> x0, blocking collectives: 15.2 us -> none  [on_device(): lax.all_gather(predicted, 'member', axis=0, tiled=True)]
    ppermute x0 -> x9, waiting for transfers between devices: none -> 12.6 us  [swap(): lax.ppermute(array, mesh_axes, [(place, place ^ offset) for place in rang...]
    ppermute x0 -> x9, starting transfers between devices: none -> 11.4 us  [swap(): lax.ppermute(array, mesh_axes, [(place, place ^ offset) for place in rang...]
    unnamed x18 -> x20, local copies, waits for them, and re-layouts: 5.34 us -> 5.13 us
  transfers between devices with their start and end apart: 2 -> 9, of which waited for: 1 -> 7; matrix products, arithmetic and copies ran while one was open for 3% -> 2% of each run, Pallas kernels for 0% -> 0%
where the time goes in v1:
time: 35.7 us; the launch traced here: 35.5 us
  waiting for transfers between devices  12.6 us (35%)
  starting transfers between devices  11.4 us (32%)
  local copies, waits for them, and re-layouts  5.73 us (16%)
  matrix products  3.6 us (10%)
  between operations  1.6 us (4%)
  other arithmetic  0.59 us (2%)
    ppermute x9, waiting for transfers between devices, swap(): lax.ppermute(array, mesh_axes, [(place, place ^ offset) for place in rang...  12.6 us
    ppermute x9, starting transfers between devices, swap(): lax.ppermute(array, mesh_axes, [(place, place ^ offset) for place in rang...  11.4 us
    unnamed x20, local copies, waits for them, and re-layouts  5.13 us
    dot_general x1, matrix products, on_device(): pre_one = jnp.dot(inputs, weight_in, preferred_element_type=jnp.float32)  1.21 us
  transfers between devices with their start and end apart: 9, of which 7 were waited for; matrix products, arithmetic and copies ran while one was open for 2% of the time, Pallas kernels for 0%

profile of v1, /device:TPU:0, one launch (start us, length us, event | category | flops | bytes accessed | tf_op | source)
XLA Modules:
  0.0 35.5 jit_solution(9719664888626761057)
XLA Ops:
  1.4 0.7 %copy-done.4 = f32[4,128]{1,0:T(4,128)S(1)} copy-done((f32[4,128]{1,0:T(4,128)S(1)}, f32[4,128]{1,0:T(4,128)}, u32[]{:S(2)}) %copy-start.4) | copy-done | bytes 2072
  2.1 1.2 %multiply_convert_fusion.1 = (bf16[1024,128]{1,0:T(8,128)(2,1)S(1)}, f32[1024,128]{1,0:T(8,128)S(1)}) fusion(f32[128]{0:T(128)S(1)} %multiply_reduce_fusion.2, bf16[1024,256]{1,0:T(8,128)(2,1)S(1)} %bitcast.44, bf16[256,128]{1,0:T(8,128)(2,1)} %param.12), kind=kOutput, calls=%fused_computation.21 | convolution fusion | flops 68419584 | bytes 1376768 | tf_op jit(solution)/shard_map/dot_general | solution.py:97
  3.4 0.3 multiply_convert_fusion
  3.7 0.3 copy-done.3
  4.0 0.2 fusion.23
  4.2 5.1 %collective-permute-start.2 = (bf16[1,8,4,256]{3,1,2,0:T(8,128)(2,1)S(1)}, bf16[1,8,4,256]{3,1,2,0:T(8,128)(2,1)S(1)}, u32[]{:S(2)}, u32[]{:S(2)}) collective-permute-start(bf16[1,8,4,256]{3,1,2,0:T(8,128)(2,1)S(1)} %convert_element_type.78), channel_id=1, source_target_pairs={{0,12},{1,13},{2,14},{3,15},{4,8},{5,9},{6,10},{7,11},{8,4},{9,5},... | collective-permute-start | bytes 49160 | tf_op jit(solution)/shard_map/ppermute | solution.py:32
  9.3 0.6 %collective-permute-start = (bf16[1,8,4,256]{3,1,2,0:T(8,128)(2,1)S(1)}, bf16[1,8,4,256]{3,1,2,0:T(8,128)(2,1)S(1)}, u32[]{:S(2)}, u32[]{:S(2)}) collective-permute-start(bf16[1,8,4,256]{3,1,2,0:T(8,128)(2,1)S(1)} %convert_element_type.78), channel_id=1, source_target_pairs={{0,4},{1,5},{2,6},{3,7},{4,0},{5,1},{6,2},{7,3},{8,12},{9,13},{10,... | collective-permute-start | bytes 49160 | tf_op jit(solution)/shard_map/ppermute | solution.py:32
  10.0 0.7 %copy-done.2 = s32[1,4,256]{2,1,0:T(4,128)S(1)} copy-done((s32[1,4,256]{2,1,0:T(4,128)S(1)}, s32[1,4,256]{2,1,0:T(4,128)}, u32[]{:S(2)}) %copy-start.2) | copy-done | bytes 4120
  10.8 0.3 collective-permute-done.2
  11.0 2.9 %collective-permute-done.1 = bf16[1,8,4,256]{3,1,2,0:T(8,128)(2,1)S(1)} collective-permute-done((bf16[1,8,4,256]{3,1,2,0:T(8,128)(2,1)S(1)}, bf16[1,8,4,256]{3,1,2,0:T(8,128)(2,1)S(1)}, u32[]{:S(2)}, u32[]{:S(2)}) %collective-permute-start.1) | collective-permute-done | bytes 16416 | tf_op jit(solution)/shard_map/ppermute | solution.py:32
  14.0 0.3 fusion.25
  14.3 0.5 %fusion = bf16[1024,128]{1,0:T(8,128)(2,1)S(1)} fusion(bf16[8,1024]{1,0:T(8,128)(2,1)S(1)} %multiply_convert_fusion.2, bf16[128,8]{0,1:T(8,128)(2,1)S(1)} %copy-done.3, f32[1024,128]{1,0:T(8,128)S(1)} %get-tuple-element.32), kind=kOutput, calls=%fused_computation.1 | convolution fusion | flops 4587520 | bytes 804864 | tf_op jit(solution)/shard_map/dot_general | solution.py:133
  14.8 0.3 fusion.24
  15.1 0.3 multiply_reduce_fusion
  15.4 0.6 %convolution_bitcast_fusion = f32[256,128]{0,1:T(8,128)S(1)} fusion(bf16[1024,256]{1,0:T(8,128)(2,1)S(1)} %bitcast.45, f32[1024,128]{1,0:T(8,128)S(1)} %get-tuple-element.30, f32[1024,128]{1,0:T(8,128)S(1)} %get-tuple-element.34, f32[128]{0:T(128)S(1)} %multiply_reduce_fusion.2), kind=kOutput, calls=%fused_computation.2 | convolution fusion | flops 69730304 | bytes 1704448 | tf_op jit(solution)/shard_map/dot_general | solution.py:145
  16.0 0.1 copy.43
  16.2 0.1 concatenate.11
  16.5 1.3 %collective-permute-done.3 = f32[208,128]{0,1:T(8,128)S(1)} collective-permute-done((f32[208,128]{0,1:T(8,128)S(1)}, f32[208,128]{0,1:T(8,128)S(1)}, u32[]{:S(2)}, u32[]{:S(2)}) %collective-permute-start.3) | collective-permute-done | bytes 106528 | tf_op jit(solution)/shard_map/ppermute | solution.py:32
  17.9 0.9 %collective-permute-start.6 = (bf16[208,128]{0,1:T(8,128)(2,1)S(1)}, bf16[208,128]{0,1:T(8,128)(2,1)S(1)}, u32[]{:S(2)}, u32[]{:S(2)}) collective-permute-start(bf16[208,128]{0,1:T(8,128)(2,1)S(1)} %add_convert_fusion.1), channel_id=1, source_target_pairs={{0,6},{1,7},{2,4},{3,5},{4,2},{5,3},{6,0},{7,1},{8,14},{9,15},{10,... | collective-permute-start | bytes 159752 | tf_op jit(solution)/shard_map/ppermute | solution.py:32
  18.8 1.6 %collective-permute-start.5 = (bf16[208,128]{0,1:T(8,128)(2,1)S(1)}, bf16[208,128]{0,1:T(8,128)(2,1)S(1)}, u32[]{:S(2)}, u32[]{:S(2)}) collective-permute-start(bf16[208,128]{0,1:T(8,128)(2,1)S(1)} %add_convert_fusion.1), channel_id=1, source_target_pairs={{0,5},{1,4},{2,7},{3,6},{4,1},{5,0},{6,3},{7,2},{8,13},{9,12},{10,... | collective-permute-start | bytes 159752 | tf_op jit(solution)/shard_map/ppermute | solution.py:32
  20.4 0.8 %collective-permute-start.4 = (bf16[208,128]{0,1:T(8,128)(2,1)S(1)}, bf16[208,128]{0,1:T(8,128)(2,1)S(1)}, u32[]{:S(2)}, u32[]{:S(2)}) collective-permute-start(bf16[208,128]{0,1:T(8,128)(2,1)S(1)} %add_convert_fusion.1), channel_id=1, source_target_pairs={{0,3},{1,2},{2,1},{3,0},{4,7},{5,6},{6,5},{7,4},{8,11},{9,10},{10,... | collective-permute-start | bytes 159752 | tf_op jit(solution)/shard_map/ppermute | solution.py:32
  21.2 2.6 %collective-permute-done.6 = bf16[208,128]{0,1:T(8,128)(2,1)S(1)} collective-permute-done((bf16[208,128]{0,1:T(8,128)(2,1)S(1)}, bf16[208,128]{0,1:T(8,128)(2,1)S(1)}, u32[]{:S(2)}, u32[]{:S(2)}) %collective-permute-start.6) | collective-permute-done | bytes 53280 | tf_op jit(solution)/shard_map/ppermute | solution.py:32
  23.8 0.6 %collective-permute-done.4 = bf16[208,128]{0,1:T(8,128)(2,1)S(1)} collective-permute-done((bf16[208,128]{0,1:T(8,128)(2,1)S(1)}, bf16[208,128]{0,1:T(8,128)(2,1)S(1)}, u32[]{:S(2)}, u32[]{:S(2)}) %collective-permute-start.4) | collective-permute-done | bytes 53280 | tf_op jit(solution)/shard_map/ppermute | solution.py:32
  24.5 2.1 %collective-permute-start.7 = (bf16[208,128]{0,1:T(8,128)(2,1)S(1)}, bf16[208,128]{0,1:T(8,128)(2,1)S(1)}, u32[]{:S(2)}, u32[]{:S(2)}) collective-permute-start(bf16[208,128]{0,1:T(8,128)(2,1)S(1)} %add_convert_fusion), channel_id=1, source_target_pairs={{0,9},{1,8},{2,11},{3,10},{4,13},{5,12},{6,15},{7,14},{8,1},{9,0},... | collective-permute-start | bytes 159752 | tf_op jit(solution)/shard_map/ppermute | solution.py:32
  26.6 4.3 %collective-permute-done.7 = bf16[208,128]{0,1:T(8,128)(2,1)S(1)} collective-permute-done((bf16[208,128]{0,1:T(8,128)(2,1)S(1)}, bf16[208,128]{0,1:T(8,128)(2,1)S(1)}, u32[]{:S(2)}, u32[]{:S(2)}) %collective-permute-start.7) | collective-permute-done | bytes 53280 | tf_op jit(solution)/shard_map/ppermute | solution.py:32
  30.9 0.2 collective-permute-start.8
  31.1 0.6 %copy.44 = f32[1,8,1,256]{3,2,1,0:T(1,128)} copy(f32[1,8,1,256]{3,1,2,0:T(8,128)S(1)} %bitcast_multiply_fusion) | data formatting | bytes 16384
  31.7 0.6 %collective-permute-done.8 = f32[208,128]{0,1:T(8,128)S(1)} collective-permute-done((f32[208,128]{0,1:T(8,128)S(1)}, f32[208,128]{0,1:T(8,128)S(1)}, u32[]{:S(2)}, u32[]{:S(2)}) %collective-permute-start.8) | collective-permute-done | bytes 106528 | tf_op jit(solution)/shard_map/ppermute | solution.py:32
  32.7 0.8 %copy.45 = f32[256,128]{1,0:T(8,128)} copy(f32[256,128]{0,1:T(8,128)S(1)} %pad_maximum_fusion) | data formatting | bytes 262144
  33.5 0.7 %copy.48 = f32[4,128]{1,0:T(4,128)} copy(f32[4,128]{0,1:T(8,128)S(1)} %slice.18) | data formatting | bytes 4096
  34.1 0.7 %copy.47 = f32[128,8]{0,1:T(8,128)} copy(f32[128,8]{1,0:T(8,128)S(1)} %slice_bitcast_fusion) | data formatting | bytes 8192
  34.8 0.7 %copy.46 = f32[128,128]{1,0:T(8,128)} copy(f32[128,128]{0,1:T(8,128)S(1)} %slice.16) | data formatting | bytes 131072
  (43 shorter events, 1.1 us)
Async XLA Ops:
  0.6 1.5 %copy-start = (bf16[1,1,4,256,256]{4,3,2,1,0:T(8,128)(2,1)S(1)}, bf16[1,1,4,256,256]{4,3,2,1,0:T(8,128)(2,1)}, u32[]{:S(2)}) copy-start(bf16[1,1,4,256,256]{4,3,2,1,0:T(8,128)(2,1)} %param.8) | copy-start | bytes 1572868
  1.3 0.7 %copy-start.4 = (f32[4,128]{1,0:T(4,128)S(1)}, f32[4,128]{1,0:T(4,128)}, u32[]{:S(2)}) copy-start(f32[4,128]{1,0:T(4,128)} %param.15) | copy-start | bytes 6148
  2.1 1.2 %copy-start.5 = (bf16[128,128]{1,0:T(8,128)(2,1)S(1)}, bf16[128,128]{1,0:T(8,128)(2,1)}, u32[]{:S(2)}) copy-start(bf16[128,128]{1,0:T(8,128)(2,1)} %param.13) | copy-start | bytes 98308
  3.3 0.7 %copy-start.3 = (bf16[128,8]{0,1:T(8,128)(2,1)S(1)}, bf16[128,8]{0,1:T(8,128)(2,1)}, u32[]{:S(2)}) copy-start(bf16[128,8]{0,1:T(8,128)(2,1)} %param.14) | copy-start | bytes 6148
  4.2 6.5 %copy-start.1 = (f32[1,8,4,256]{3,2,1,0:T(4,128)S(1)}, f32[1,8,4,256]{3,2,1,0:T(4,128)}, u32[]{:S(2)}) copy-start(f32[1,8,4,256]{3,2,1,0:T(4,128)} %param.9) | copy-start | bytes 98308
  4.2 6.8 %collective-permute-start.2 = (bf16[1,8,4,256]{3,1,2,0:T(8,128)(2,1)S(1)}, bf16[1,8,4,256]{3,1,2,0:T(8,128)(2,1)S(1)}, u32[]{:S(2)}, u32[]{:S(2)}) collective-permute-start(bf16[1,8,4,256]{3,1,2,0:T(8,128)(2,1)S(1)} %convert_element_type.78), channel_id=1, source_target_pairs={{0,12},{1,13},{2,14},{3,15},{4,8},{5,9},{6,10},{7,11},{8,4},{9,5},... | collective-permute-start | bytes 49160 | tf_op jit(solution)/shard_map/ppermute | solution.py:32
  9.3 4.6 %collective-permute-start.1 = (bf16[1,8,4,256]{3,1,2,0:T(8,128)(2,1)S(1)}, bf16[1,8,4,256]{3,1,2,0:T(8,128)(2,1)S(1)}, u32[]{:S(2)}, u32[]{:S(2)}) collective-permute-start(bf16[1,8,4,256]{3,1,2,0:T(8,128)(2,1)S(1)} %convert_element_type.78), channel_id=1, source_target_pairs={{0,8},{1,9},{2,10},{3,11},{4,12},{5,13},{6,14},{7,15},{8,0},{9,1},... | collective-permute-start | bytes 49160 | tf_op jit(solution)/shard_map/ppermute | solution.py:32
  9.3 4.6 %collective-permute-start = (bf16[1,8,4,256]{3,1,2,0:T(8,128)(2,1)S(1)}, bf16[1,8,4,256]{3,1,2,0:T(8,128)(2,1)S(1)}, u32[]{:S(2)}, u32[]{:S(2)}) collective-permute-start(bf16[1,8,4,256]{3,1,2,0:T(8,128)(2,1)S(1)} %convert_element_type.78), channel_id=1, source_target_pairs={{0,4},{1,5},{2,6},{3,7},{4,0},{5,1},{6,2},{7,3},{8,12},{9,13},{10,... | collective-permute-start | bytes 49160 | tf_op jit(solution)/shard_map/ppermute | solution.py:32
  10.0 0.7 %copy-start.2 = (s32[1,4,256]{2,1,0:T(4,128)S(1)}, s32[1,4,256]{2,1,0:T(4,128)}, u32[]{:S(2)}) copy-start(s32[1,4,256]{2,1,0:T(4,128)} %param.10) | copy-start | bytes 12292
  16.4 1.4 %collective-permute-start.3 = (f32[208,128]{0,1:T(8,128)S(1)}, f32[208,128]{0,1:T(8,128)S(1)}, u32[]{:S(2)}, u32[]{:S(2)}) collective-permute-start(f32[208,128]{0,1:T(8,128)S(1)} %constant_dynamic-slice_fusion), channel_id=1, source_target_pairs={{0,1},{1,0},{2,3},{3,2},{4,5},{5,4},{6,7},{7,6},{8,9},{9,8},{10,11... | collective-permute-start | bytes 319496 | tf_op jit(solution)/shard_map/ppermute | solution.py:32
  17.9 5.9 %collective-permute-start.6 = (bf16[208,128]{0,1:T(8,128)(2,1)S(1)}, bf16[208,128]{0,1:T(8,128)(2,1)S(1)}, u32[]{:S(2)}, u32[]{:S(2)}) collective-permute-start(bf16[208,128]{0,1:T(8,128)(2,1)S(1)} %add_convert_fusion.1), channel_id=1, source_target_pairs={{0,6},{1,7},{2,4},{3,5},{4,2},{5,3},{6,0},{7,1},{8,14},{9,15},{10,... | collective-permute-start | bytes 159752 | tf_op jit(solution)/shard_map/ppermute | solution.py:32
  18.8 5.1 %collective-permute-start.5 = (bf16[208,128]{0,1:T(8,128)(2,1)S(1)}, bf16[208,128]{0,1:T(8,128)(2,1)S(1)}, u32[]{:S(2)}, u32[]{:S(2)}) collective-permute-start(bf16[208,128]{0,1:T(8,128)(2,1)S(1)} %add_convert_fusion.1), channel_id=1, source_target_pairs={{0,5},{1,4},{2,7},{3,6},{4,1},{5,0},{6,3},{7,2},{8,13},{9,12},{10,... | collective-permute-start | bytes 159752 | tf_op jit(solution)/shard_map/ppermute | solution.py:32
  20.4 4.0 %collective-permute-start.4 = (bf16[208,128]{0,1:T(8,128)(2,1)S(1)}, bf16[208,128]{0,1:T(8,128)(2,1)S(1)}, u32[]{:S(2)}, u32[]{:S(2)}) collective-permute-start(bf16[208,128]{0,1:T(8,128)(2,1)S(1)} %add_convert_fusion.1), channel_id=1, source_target_pairs={{0,3},{1,2},{2,1},{3,0},{4,7},{5,6},{6,5},{7,4},{8,11},{9,10},{10,... | collective-permute-start | bytes 159752 | tf_op jit(solution)/shard_map/ppermute | solution.py:32
  24.5 6.4 %collective-permute-start.7 = (bf16[208,128]{0,1:T(8,128)(2,1)S(1)}, bf16[208,128]{0,1:T(8,128)(2,1)S(1)}, u32[]{:S(2)}, u32[]{:S(2)}) collective-permute-start(bf16[208,128]{0,1:T(8,128)(2,1)S(1)} %add_convert_fusion), channel_id=1, source_target_pairs={{0,9},{1,8},{2,11},{3,10},{4,13},{5,12},{6,15},{7,14},{8,1},{9,0},... | collective-permute-start | bytes 159752 | tf_op jit(solution)/shard_map/ppermute | solution.py:32
  30.9 1.4 %collective-permute-start.8 = (f32[208,128]{0,1:T(8,128)S(1)}, f32[208,128]{0,1:T(8,128)S(1)}, u32[]{:S(2)}, u32[]{:S(2)}) collective-permute-start(f32[208,128]{0,1:T(8,128)S(1)} %convert_add_fusion), channel_id=1, source_target_pairs={{0,1},{1,0},{2,3},{3,2},{4,5},{5,4},{6,7},{7,6},{8,9},{9,8},{10,11... | collective-permute-start | bytes 319496 | tf_op jit(solution)/shard_map/ppermute | solution.py:32

commit v2 on v0

v2 whole, which is shorter than its diff:
```python
import functools
import math

import jax
import jax.numpy as jnp
from jax import lax
from jax.experimental import pallas as pl
from jax.experimental.pallas import tpu as pltpu
from jax.sharding import PartitionSpec as P

gelu_coef = 0.7978845608028654
cubic_coef = 0.044715
soft_square = 0.0625
mesh_axes = ("member", "tile", "sample")
row_block = 8
point_chunk = 512
f32 = jnp.float32
bf16 = jnp.bfloat16


def rise_of(values):
    inner = jnp.tanh(values * (gelu_coef + gelu_coef * cubic_coef * (values * values)))
    return 0.5 + 0.5 * inner


def slope_of(values, rise):
    inside = values * (2.0 * gelu_coef + 6.0 * gelu_coef * cubic_coef * (values * values))
    return rise + rise * (1.0 - rise) * inside


def soft(values):
    return jnp.sqrt(values * values + soft_square)


def soft_slope(values):
    return values * lax.rsqrt(values * values + soft_square)


def forward_kernel(
    chunk, order, latent, observed, radar_valid, weight_in, weight_mid, weight_out, gains,
    latent_copy, observed_copy, valid_copy, pre_one, rise_one, hidden_one, pre_two, rise_two, hidden_two,
    predicted, sent, gain_row, mid_at, out_at, in_at, gains_at, sems, chunk_sems,
):
    block = latent_copy.shape[0]
    rows = observed_copy.shape[1]
    step = pl.program_id(0)
    here = pl.ds(pl.multiple_of(step * rows, rows), rows)
    pieces = []
    for number in range(block // chunk):
        source = latent.at[pl.ds(pl.multiple_of(step * block + number * chunk, chunk), chunk), :]
        into = latent_copy.at[pl.ds(number * chunk, chunk), :]
        pieces.append(pltpu.make_async_copy(source, into, chunk_sems.at[number]))
    pairs = [
        (weight_in, in_at), (gains, gains_at), (weight_mid, mid_at), (weight_out, out_at),
        (observed.at[:, here, :], observed_copy), (radar_valid.at[here, :], valid_copy),
    ]
    copies = [pltpu.make_async_copy(source, into, sems.at[k]) for k, (source, into) in enumerate(pairs)]
    copies[0].start()
    pieces[0].start()
    for copy in copies[1:4] + pieces[1:] + copies[4:]:
        copy.start()
    for number, piece in enumerate(pieces):
        spot = slice(number * chunk, (number + 1) * chunk)
        if number == 0:
            copies[0].wait()
        piece.wait()
        first = jnp.dot(latent_copy[spot, :], in_at[...], preferred_element_type=f32)
        rise = rise_of(first)
        if number == 0:
            for copy in copies[1:4]:
                copy.wait()
            gain = gains_at[pl.ds(order[0, 0], 1), :]
            gain_row[...] = gain
        pre_one[spot, :] = first
        rise_one[spot, :] = rise
        one = (first * rise * gain).astype(bf16)
        hidden_one[spot, :] = one
        second = jnp.dot(one, mid_at[...], preferred_element_type=f32)
        rise = rise_of(second)
        pre_two[spot, :] = second
        rise_two[spot, :] = rise
        two = (second * rise).astype(bf16)
        hidden_two[spot, :] = two
        last = lax.dot_general(out_at[...], two, (((1,), (1,)), ((), ())), preferred_element_type=f32)
        predicted[:, spot] = last
        sent[:, spot] = last.astype(bf16)
    for copy in copies[4:]:
        copy.wait()


def derivative_kernel(
    latent, observed, radar_valid, pre_one, rise_one, hidden_one, pre_two, rise_two, gain_row,
    act_one, slope_one, slope_two, latent_t, hidden_t, target, valid,
):
    cols = observed.shape[2]
    for row in range(observed.shape[1]):
        spot = slice(row * cols, (row + 1) * cols)
        target[:, spot] = observed[:, row, :]
        valid[:, spot] = radar_valid[row : row + 1, :].astype(f32)
    latent_t[...] = latent[...].T
    hidden_t[...] = hidden_one[...].T
    act_one[...] = pre_one[...] * rise_one[...]
    slope_one[...] = slope_of(pre_one[...], rise_one[...]) * gain_row[...]
    slope_two[...] = slope_of(pre_two[...], rise_two[...])


def backward_kernel(steps, scale_own, scale_pair, parts, order, *refs):
    (predicted, target, valid), refs = refs[:3], refs[3:]
    ensemble, refs = refs[:parts], refs[parts:]
    (latent_t, hidden_t, hidden_two, act_one, slope_one, slope_two, weight_mid, weight_out), refs = refs[:8], refs[8:]
    keep, away, rows = refs
    width, hidden = latent_t.shape[0], hidden_t.shape[0]
    fields = predicted.shape[0]
    half = keep.shape[0]
    step = pl.program_id(0)

    def put(first, count, value):
        if steps == 1:
            rows[first : first + count, :] = value
        else:
            rows[first : first + count, :] += value

    if steps > 1:

        @pl.when(step == 0)
        def _():
            rows[...] = jnp.zeros_like(rows)

    mine = predicted[...]
    slopes = None
    for part in ensemble:
        for k in range(part.shape[0]):
            one = soft_slope(mine - part[k].astype(f32))
            slopes = one if slopes is None else slopes + one
    grad = valid[...] * (soft_slope(mine - target[...]) * scale_own - slopes * scale_pair)
    flat = grad.astype(bf16)
    put(width + hidden, fields, jnp.dot(flat, hidden_two[...], preferred_element_type=f32))
    grad_hid_two = lax.dot_general(
        flat, weight_out[...], (((0,), (0,)), ((), ())), preferred_element_type=f32
    )
    grad_pre_two = (grad_hid_two * slope_two[...]).astype(bf16)
    grad_hid_one = lax.dot_general(
        grad_pre_two, weight_mid[...], (((1,), (1,)), ((), ())), preferred_element_type=f32
    )
    grad_pre_one = (grad_hid_one * slope_one[...]).astype(bf16)
    put(0, width, jnp.dot(latent_t[...], grad_pre_one, preferred_element_type=f32))
    put(width, hidden, jnp.dot(hidden_t[...], grad_pre_two, preferred_element_type=f32))
    gain_row = jnp.sum(grad_hid_one * act_one[...], axis=0, keepdims=True)
    first = width + hidden + fields
    count = rows.shape[0] - first
    spots = lax.broadcasted_iota(jnp.int32, (count, 1), 0)
    put(first, count, jnp.where(spots == order[0, 0], gain_row, 0.0))

    @pl.when(step == steps - 1)
    def _():
        which = half_of_device()
        keep[...] = rows[pl.ds(pl.multiple_of(which * half, 16), half), :]
        away[...] = rows[pl.ds(pl.multiple_of((1 - which) * half, 16), half), :]


def score_kernel(parts, predicted, target, valid, *refs):
    ensemble, score = refs[:parts], refs[parts]
    fields, rows, cols = score.shape
    here = pl.ds(pl.multiple_of(lax.axis_index("member") * (rows * cols), 128), rows * cols)
    blocks = [predicted[:, here]]
    for part in ensemble:
        for k in range(part.shape[0]):
            blocks.append(part[k, :, here].astype(f32))
    members = len(blocks)
    skill = sum(soft(block - target[:, here]) for block in blocks)
    if members <= 8:
        pairs = sum(soft(blocks[i] - blocks[j]) for i in range(members) for j in range(i))
    else:
        stack = jnp.stack(blocks)
        pairs = sum(jnp.sum(soft(stack[i + 1 :] - blocks[i]), axis=0) for i in range(members - 1))
    spread = 2.0 * pairs + members * math.sqrt(soft_square)
    value = valid[:, here] * (skill / members - spread / (2.0 * members * (members - 1)))
    for row in range(rows):
        score[:, row, :] = value[:, row * cols : (row + 1) * cols]


def output_kernel(total, other, grad_in, grad_mid, grad_out, grad_gains, sems):
    half = total.shape[0]
    moves = []
    first = 0
    for target in (grad_in, grad_mid, grad_out, grad_gains):
        last = first + target.shape[0]
        for side in range(2):
            low, high = max(first, side * half), min(last, (side + 1) * half)
            if low < high:
                moves.append((target, side, low - side * half, low - first, high - low))
        first = last

    def send(halves):
        copies = []
        for number, (target, side, source, into, count) in enumerate(moves):
            copy = pltpu.make_async_copy(
                halves[side].at[pl.ds(source, count), :], target.at[pl.ds(into, count), :], sems.at[number]
            )
            copy.start()
            copies.append(copy)
        for copy in copies:
            copy.wait()

    which = half_of_device()

    @pl.when(which == 0)
    def _():
        send((total, other))

    @pl.when(which != 0)
    def _():
        send((other, total))


def swap(array, offset):
    count = 1
    for axis in mesh_axes:
        count *= lax.axis_size(axis)
    return lax.ppermute(array, mesh_axes, [(place, place ^ offset) for place in range(count)])


def rounds_of(bits):
    return [bits[first : first + 2] for first in range(0, len(bits), 2)]


def bits_of(size, lowest):
    assert size & (size - 1) == 0
    return [lowest << place for place in range(size.bit_length() - 1)]


def gather_members(block):
    unit = lax.axis_size("tile") * lax.axis_size("sample")
    parts = [block[None]]
    for bits in rounds_of(bits_of(lax.axis_size("member"), unit)):
        whole = parts[0] if len(parts) == 1 else jnp.concatenate(parts)
        offsets = bits if len(bits) == 1 else [bits[0], bits[1], bits[0] ^ bits[1]]
        parts = parts + [swap(whole, offset) for offset in offsets]
    return parts[1:]


def reduction_bits():
    tiles, samples = lax.axis_size("tile"), lax.axis_size("sample")
    return bits_of(tiles, samples) + bits_of(lax.axis_size("member"), samples * tiles)


def half_of_device():
    place = lax.axis_index(mesh_axes)
    which = place & 1
    for bit in reduction_bits():
        which = which ^ jnp.where(place & bit, 1, 0)
    return which


def sum_parameters(keep, away, link_dtype):
    total = keep + swap(away, 1)
    for group in rounds_of(reduction_bits()):
        sent = total.astype(link_dtype)
        if len(group) == 1:
            arrived = swap(sent, group[0] ^ 1)
            total = sent.astype(f32) + arrived.astype(f32)
        else:
            near, far = group
            parts = [swap(sent, near ^ 1), swap(sent, far ^ 1), swap(sent, near ^ far)]
            parts = [part.astype(f32) for part in parts]
            total = (sent.astype(f32) + parts[0]) + (parts[1] + parts[2])
    return total, swap(total, 1)


def whole_spec(array):
    return pl.BlockSpec(array.shape, lambda step: (0,) * len(array.shape))


def block_spec(shape, block, axis):
    sizes = tuple(block if place == axis else size for place, size in enumerate(shape))
    return pl.BlockSpec(sizes, lambda step: tuple(step if place == axis else 0 for place in range(len(sizes))))


smem = pl.BlockSpec(memory_space=pltpu.SMEM)
kernel_params = pltpu.CompilerParams(vmem_limit_bytes=24 * 1024 * 1024)


def on_device(
    latent, observed, radar_valid, member_order, weight_in, weight_mid, weight_out, gains
):
    row_count = latent.shape[2]
    tile_cols = latent.shape[3]
    width = latent.shape[4]
    fields = weight_out.shape[1]
    hidden = weight_mid.shape[0]
    members = lax.axis_size("member")
    col_count = tile_cols * lax.axis_size("tile")
    points = row_count * tile_cols
    block_rows = min(row_count, row_block)
    block = block_rows * tile_cols
    steps = row_count // block_rows
    norm_factor = 1.0 / math.sqrt(lax.axis_size("sample") * row_count * col_count)
    inputs = latent[0, 0].reshape(points, width)
    weight_out_t = weight_out.T
    chunk = min(block, point_chunk)

    by_point = lambda shape: block_spec(shape, block, 0)
    by_lane = lambda shape: block_spec(shape, block, len(shape) - 1)
    result = pltpu.VMEM if steps == 1 else jax.ShapeDtypeStruct
    tall = lambda dtype: result((points, hidden), dtype)
    wide = lambda size, dtype: result((size, points), dtype)
    tall_spec = by_point((points, hidden))
    wide_spec = by_lane((fields, points))
    observed_spec = block_spec((fields, row_count, tile_cols), block_rows, 1)
    valid_spec = block_spec((row_count, tile_cols), block_rows, 0)
    gain_shape = result((1, hidden), f32)

    (latent_copy, observed_copy, valid_copy, pre_one, rise_one, hidden_one, pre_two, rise_two, hidden_two,
     predicted, sent, gain_row, mid_copy, out_copy) = pl.pallas_call(
        functools.partial(forward_kernel, chunk),
        grid=(steps,),
        in_specs=[smem] + [pl.BlockSpec(memory_space=pltpu.HBM)] * 7,
        out_specs=[by_point((points, width)), observed_spec, valid_spec]
        + [tall_spec] * 6 + [wide_spec] * 2
        + [whole_spec(array) for array in (gain_shape, weight_mid, weight_out_t)],
        out_shape=[
            result((points, width), bf16),
            result((fields, row_count, tile_cols), f32),
            result((row_count, tile_cols), jnp.int32),
            tall(f32), tall(f32), tall(bf16), tall(f32), tall(f32), tall(bf16),
            wide(fields, f32), wide(fields, bf16), gain_shape,
            result(weight_mid.shape, bf16), result(weight_out_t.shape, bf16),
        ],
        scratch_shapes=[pltpu.VMEM(array.shape, array.dtype) for array in (weight_in, gains)]
        + [pltpu.SemaphoreType.DMA((6,)), pltpu.SemaphoreType.DMA((block // chunk,))],
        compiler_params=kernel_params,
        name="forward",
    )(member_order, *[
        pltpu.with_memory_space_constraint(array, pltpu.HBM)
        for array in (inputs, observed[0], radar_valid[0], weight_in, weight_mid, weight_out_t, gains)
    ])

    parts = gather_members(sent)

    act_one, slope_one, slope_two, latent_t, hidden_t, target, is_valid = pl.pallas_call(
        derivative_kernel,
        grid=(steps,),
        in_specs=[by_point((points, width)), observed_spec, valid_spec]
        + [tall_spec] * 5 + [whole_spec(gain_shape)],
        out_specs=[tall_spec] * 3 + [by_lane((size, points)) for size in (width, hidden, fields, 1)],
        out_shape=[tall(f32)] * 3 + [wide(width, bf16), wide(hidden, bf16), wide(fields, f32), wide(1, f32)],
        compiler_params=kernel_params,
        name="derivatives",
    )(latent_copy, observed_copy, valid_copy, pre_one, rise_one, hidden_one, pre_two, rise_two, gain_row)

    used = width + hidden + fields + members
    half = -(-used // 32) * 16
    half_shape = jax.ShapeDtypeStruct((half, hidden), f32)
    keep, away = pl.pallas_call(
        functools.partial(
            backward_kernel,
            steps,
            norm_factor / members,
            norm_factor / (members * (members - 1.0)),
            len(parts),
        ),
        grid=(steps,),
        in_specs=[smem, wide_spec, wide_spec, by_lane((1, points))]
        + [by_lane(part.shape) for part in parts]
        + [by_lane((width, points)), by_lane((hidden, points))]
        + [tall_spec] * 4
        + [whole_spec(weight_mid), whole_spec(weight_out_t)],
        out_specs=[whole_spec(half_shape)] * 2,
        out_shape=[half_shape] * 2,
        scratch_shapes=[pltpu.VMEM((2 * half, hidden), f32)],
        compiler_params=kernel_params,
        name="backward",
    )(
        member_order, predicted, target, is_valid, *parts, latent_t, hidden_t,
        hidden_two, act_one, slope_one, slope_two, mid_copy, out_copy,
    )

    score_shape = jax.ShapeDtypeStruct((fields, row_count // members, tile_cols), f32)
    score_inputs = (predicted, target, is_valid, *parts)
    pixel_score = pl.pallas_call(
        functools.partial(score_kernel, len(parts)),
        grid=(1,),
        in_specs=[whole_spec(array) for array in score_inputs],
        out_specs=whole_spec(score_shape),
        out_shape=score_shape,
        compiler_params=kernel_params,
        name="score",
    )(*score_inputs)

    total, other = sum_parameters(keep, away, bf16)
    shapes = [jax.ShapeDtypeStruct((size, hidden), f32) for size in (width, hidden, fields, members)]
    grad_in, grad_mid, grad_out_t, grad_gains = pl.pallas_call(
        output_kernel,
        grid=(1,),
        in_specs=[whole_spec(total), whole_spec(other)],
        out_specs=[pl.BlockSpec(memory_space=pltpu.HBM)] * 4,
        out_shape=shapes,
        scratch_shapes=[pltpu.SemaphoreType.DMA((8,))],
        compiler_params=kernel_params,
        name="gradients",
    )(total, other)
    return (pixel_score[None], grad_in, grad_mid, grad_out_t.T, grad_gains)


def solution(mesh):
    placed = (
        P(("group", "sample"), "member", None, "tile", None),
        P(("group", "sample"), None, None, "tile"),
        P(("group", "sample"), None, "tile"),
        P(("group", "sample"), "member"),
        P(),
        P(),
        P(),
        P(),
    )
    return jax.shard_map(
        on_device,
        mesh=mesh,
        in_specs=placed,
        out_specs=(
            P(("group", "sample"), None, "member", "tile"),
            P("group", None),
            P("group", None),
            P("group", None),
            P("group", None),
        ),
        check_vma=False,
    )
```

time: 134 us -> 29.7 us (0.22)
  waiting for transfers between devices: 60 us -> 9.65 us
  blocking collectives: 46.7 us -> 0 us
  between operations: 16.3 us -> 1.33 us
  starting transfers between devices: 0.08 us -> 13 us
  Pallas kernels: 0 us -> 5.44 us
  local copies, waits for them, and re-layouts: 5.34 us -> 0 us
  matrix products: 4.76 us -> 0 us
    psum x1 -> x0, waiting for transfers between devices: 60 us -> none  [on_device(): lax.psum((grad_in, grad_mid, grad_out, grad_gains), ('member', 'tile', 's...]
    psum x1 -> x0, blocking collectives: 31.5 us -> none  [on_device(): lax.psum((grad_in, grad_mid, grad_out, grad_gains), ('member', 'tile', 's...]
    all_gather x1 -> x0, blocking collectives: 15.2 us -> none  [on_device(): lax.all_gather(predicted, 'member', axis=0, tiled=True)]
    ppermute x0 -> x9, starting transfers between devices: none -> 13 us  [swap(): lax.ppermute(array, mesh_axes, [(place, place ^ offset) for place in rang...]
    ppermute x0 -> x9, waiting for transfers between devices: none -> 9.65 us  [swap(): lax.ppermute(array, mesh_axes, [(place, place ^ offset) for place in rang...]
    pallas_call x0 -> x5, Pallas kernels: none -> 5.44 us  [the longest x1 2.37 us: on_device(): pl.pallas_call(functools.partial(forward_kernel, chunk), grid=(steps,), i...]
    unnamed x18 -> x0, local copies, waits for them, and re-layouts: 5.34 us -> none
    dot_general x8 -> x0, matrix products: 4.76 us -> none  [the longest x1 1.21 us: on_device(): lax.dot_general(inputs, grad_pre_one, (((0,), (0,)), ((), ())), preferred...]
  transfers between devices with their start and end apart: 2 -> 9, of which waited for: 1 -> 7; matrix products, arithmetic and copies ran while one was open for 3% -> 0% of each run, Pallas kernels for 0% -> 5%
where the time goes in v2:
time: 29.7 us; the launch traced here: 29.5 us
  starting transfers between devices  13 us (44%)
  waiting for transfers between devices  9.65 us (32%)
  Pallas kernels  5.44 us (18%)
  between operations  1.33 us (4%)
    ppermute x9, starting transfers between devices, swap(): lax.ppermute(array, mesh_axes, [(place, place ^ offset) for place in rang...  13 us
    ppermute x9, waiting for transfers between devices, swap(): lax.ppermute(array, mesh_axes, [(place, place ^ offset) for place in rang...  9.65 us
    pallas_call x1, Pallas kernels, on_device(): pl.pallas_call(functools.partial(forward_kernel, chunk), grid=(steps,), i...  2.37 us
    pallas_call x1, Pallas kernels, on_device(): pl.pallas_call(derivative_kernel, grid=(steps,), in_specs=[by_point((poin...  0.94 us
    pallas_call x1, Pallas kernels, on_device(): pl.pallas_call(functools.partial(backward_kernel, steps, norm_factor / me...  0.75 us
    pallas_call x1, Pallas kernels, on_device(): pl.pallas_call(output_kernel, grid=(1,), in_specs=[whole_spec(total), who...  0.74 us
    pallas_call x1, Pallas kernels, on_device(): pl.pallas_call(functools.partial(score_kernel, len(parts)), grid=(1,), in...  0.64 us
  transfers between devices with their start and end apart: 9, of which 7 were waited for; matrix products, arithmetic and copies ran while one was open for 0% of the time, Pallas kernels for 5%

profile of v2, /device:TPU:0, one launch (start us, length us, event | category | flops | bytes accessed | tf_op | source)
XLA Modules:
  0.0 29.5 jit_solution(7504183407692937358)
XLA Ops:
  1.3 2.4 %forward.1 = (bf16[1024,256]{1,0:T(8,128)(2,1)S(1)}, f32[8,4,256]{2,1,0:T(4,128)S(1)}, s32[4,256]{1,0:T(4,128)S(1)}, f32[1024,128]{1,0:T(8,128)S(1)}, f32[1024,1...) custom-call(s32[1,1]{1,0:T(1,128)S(6)} %copy.13.order, ...), custom_call_target="tpu_custom_call" | custom-call | tf_op jit(solution)/shard_map/forward/pallas_call | solution.py:314
  3.7 5.1 %collective-permute-start.2 = (bf16[1,8,1024]{2,1,0:T(8,128)(2,1)S(1)}, bf16[1,8,1024]{2,1,0:T(8,128)(2,1)S(1)}, u32[]{:S(2)}, u32[]{:S(2)}) collective-permute-start(bf16[1,8,1024]{2,1,0:T(8,128)(2,1)S(1)} %bitcast.7), channel_id=1, source_target_pairs={{0,12},{1,13},{2,14},{3,15},{4,8},{5,9},{6,10},{7,11},{8,4},{9,5},... | collective-permute-start | bytes 49160 | tf_op jit(solution)/shard_map/ppermute | solution.py:220
  8.8 0.0 collective-permute-start.1
  8.8 0.6 %collective-permute-start = (bf16[1,8,1024]{2,1,0:T(8,128)(2,1)S(1)}, bf16[1,8,1024]{2,1,0:T(8,128)(2,1)S(1)}, u32[]{:S(2)}, u32[]{:S(2)}) collective-permute-start(bf16[1,8,1024]{2,1,0:T(8,128)(2,1)S(1)} %bitcast.9), channel_id=1, source_target_pairs={{0,4},{1,5},{2,6},{3,7},{4,0},{5,1},{6,2},{7,3},{8,12},{9,13},{10,... | collective-permute-start | bytes 49160 | tf_op jit(solution)/shard_map/ppermute | solution.py:220
  9.4 0.9 %derivatives.1 = (f32[1024,128]{1,0:T(8,128)S(1)}, f32[1024,128]{1,0:T(8,128)S(1)}, f32[1024,128]{1,0:T(8,128)S(1)}, bf16[256,1024]{1,0:T(8,128)(2,1)S(1)}, bf16...) custom-call(bf16[1024,256]{1,0:T(8,128)(2,1)S(1)} %get-tuple-element.33.latent, ...), custom_call_target="tpu_custom_call" | custom-call | tf_op jit(solution)/shard_map/derivatives/pallas_call | solution.py:340
  10.4 0.1 collective-permute-done.2.refs_2_.refs_5_
  10.5 2.9 %collective-permute-done.1.refs_1_.refs_4_ = bf16[1,8,1024]{2,1,0:T(8,128)(2,1)S(1)} collective-permute-done((bf16[1,8,1024]{2,1,0:T(8,128)(2,1)S(1)}, bf16[1,8,1024]{2,1,0:T(8,128)(2,1)S(1)}, u32[]{:S(2)}, u32[]{:S(2)}) %collective-permute-start.1) | collective-permute-done | bytes 16416 | tf_op jit(solution)/shard_map/ppermute | solution.py:220
  13.4 0.0 collective-permute-done.refs_0_.refs_3_
  13.4 0.7 %backward.1 = (f32[208,128]{1,0:T(8,128)S(1)}, f32[208,128]{1,0:T(8,128)S(1)}) custom-call(s32[1,1]{1,0:T(1,128)S(6)} %copy.13.order, f32[8,1024]{1,0:T(8,128)S(1)} %get-tuple-element.32.predicted.refs_0_, f32[8,1024]{1,0:T(8,128)S(1)} %get-tuple-element.42.target.refs_1_, f32[1,1024]{1,0:T(1,128)S(1)} %get-tuple-element.43.valid.refs_2_, ...), custom_call_target="tpu_custom_call" | custom-call | tf_op jit(solution)/shard_map/backward/pallas_call | solution.py:354
  14.2 0.1 collective-permute-start.3
  14.2 1.3 %collective-permute-done.3 = f32[208,128]{1,0:T(8,128)S(1)} collective-permute-done((f32[208,128]{1,0:T(8,128)S(1)}, f32[208,128]{1,0:T(8,128)S(1)}, u32[]{:S(2)}, u32[]{:S(2)}) %collective-permute-start.3) | collective-permute-done | bytes 106528 | tf_op jit(solution)/shard_map/ppermute | solution.py:220
  15.6 0.9 %collective-permute-start.6 = (bf16[208,128]{1,0:T(8,128)(2,1)S(1)}, bf16[208,128]{1,0:T(8,128)(2,1)S(1)}, u32[]{:S(2)}, u32[]{:S(2)}) collective-permute-start(bf16[208,128]{1,0:T(8,128)(2,1)S(1)} %add_convert_fusion.1), channel_id=1, source_target_pairs={{0,6},{1,7},{2,4},{3,5},{4,2},{5,3},{6,0},{7,1},{8,14},{9,15},{10,... | collective-permute-start | bytes 159752 | tf_op jit(solution)/shard_map/ppermute | solution.py:220
  16.4 1.6 %collective-permute-start.5 = (bf16[208,128]{1,0:T(8,128)(2,1)S(1)}, bf16[208,128]{1,0:T(8,128)(2,1)S(1)}, u32[]{:S(2)}, u32[]{:S(2)}) collective-permute-start(bf16[208,128]{1,0:T(8,128)(2,1)S(1)} %add_convert_fusion.1), channel_id=1, source_target_pairs={{0,5},{1,4},{2,7},{3,6},{4,1},{5,0},{6,3},{7,2},{8,13},{9,12},{10,... | collective-permute-start | bytes 159752 | tf_op jit(solution)/shard_map/ppermute | solution.py:220
  18.1 0.8 %collective-permute-start.4 = (bf16[208,128]{1,0:T(8,128)(2,1)S(1)}, bf16[208,128]{1,0:T(8,128)(2,1)S(1)}, u32[]{:S(2)}, u32[]{:S(2)}) collective-permute-start(bf16[208,128]{1,0:T(8,128)(2,1)S(1)} %add_convert_fusion.1), channel_id=1, source_target_pairs={{0,3},{1,2},{2,1},{3,0},{4,7},{5,6},{6,5},{7,4},{8,11},{9,10},{10,... | collective-permute-start | bytes 159752 | tf_op jit(solution)/shard_map/ppermute | solution.py:220
  18.8 2.1 %collective-permute-done.6 = bf16[208,128]{1,0:T(8,128)(2,1)S(1)} collective-permute-done((bf16[208,128]{1,0:T(8,128)(2,1)S(1)}, bf16[208,128]{1,0:T(8,128)(2,1)S(1)}, u32[]{:S(2)}, u32[]{:S(2)}) %collective-permute-start.6) | collective-permute-done | bytes 53280 | tf_op jit(solution)/shard_map/ppermute | solution.py:220
  21.0 0.0 collective-permute-done.5
  21.0 0.6 %collective-permute-done.4 = bf16[208,128]{1,0:T(8,128)(2,1)S(1)} collective-permute-done((bf16[208,128]{1,0:T(8,128)(2,1)S(1)}, bf16[208,128]{1,0:T(8,128)(2,1)S(1)}, u32[]{:S(2)}, u32[]{:S(2)}) %collective-permute-start.4) | collective-permute-done | bytes 53280 | tf_op jit(solution)/shard_map/ppermute | solution.py:220
  21.7 2.3 %collective-permute-start.7 = (bf16[208,128]{1,0:T(8,128)(2,1)S(1)}, bf16[208,128]{1,0:T(8,128)(2,1)S(1)}, u32[]{:S(2)}, u32[]{:S(2)}) collective-permute-start(bf16[208,128]{1,0:T(8,128)(2,1)S(1)} %add_convert_fusion), channel_id=1, source_target_pairs={{0,9},{1,8},{2,11},{3,10},{4,13},{5,12},{6,15},{7,14},{8,1},{9,0},... | collective-permute-start | bytes 159752 | tf_op jit(solution)/shard_map/ppermute | solution.py:220
  24.0 2.2 %collective-permute-done.7 = bf16[208,128]{1,0:T(8,128)(2,1)S(1)} collective-permute-done((bf16[208,128]{1,0:T(8,128)(2,1)S(1)}, bf16[208,128]{1,0:T(8,128)(2,1)S(1)}, u32[]{:S(2)}, u32[]{:S(2)}) %collective-permute-start.7) | collective-permute-done | bytes 53280 | tf_op jit(solution)/shard_map/ppermute | solution.py:220
  26.2 1.6 %collective-permute-start.8 = (f32[208,128]{1,0:T(8,128)S(1)}, f32[208,128]{1,0:T(8,128)S(1)}, u32[]{:S(2)}, u32[]{:S(2)}) collective-permute-start(f32[208,128]{1,0:T(8,128)S(1)} %convert_add_fusion.total), channel_id=1, source_target_pairs={{0,1},{1,0},{2,3},{3,2},{4,5},{5,4},{6,7},{7,6},{8,9},{9,8},{10,11... | collective-permute-start | bytes 319496 | tf_op jit(solution)/shard_map/ppermute | solution.py:220
  27.8 0.6 %score.1 = f32[8,1,256]{2,1,0:T(1,128)} custom-call(f32[8,1024]{1,0:T(8,128)S(1)} %get-tuple-element.32.predicted.refs_0_, f32[8,1024]{1,0:T(8,128)S(1)} %get-tuple-element.42.target.refs_1_, f32[1,1024]{1,0:T(1,128)S(1)} %get-tuple-element.43.valid.refs_2_, bf16[1,8,1024]{2,1,0:T(8,128)(2,1)S(1)} %collective-permute-done.refs_0_.refs_3_, ...), custom_call_target="tpu_custom_call" | custom-call | tf_op jit(solution)/shard_map/score/pallas_call | solution.py:380
  28.4 0.3 %collective-permute-done.8.other = f32[208,128]{1,0:T(8,128)S(1)} collective-permute-done((f32[208,128]{1,0:T(8,128)S(1)}, f32[208,128]{1,0:T(8,128)S(1)}, u32[]{:S(2)}, u32[]{:S(2)}) %collective-permute-start.8) | collective-permute-done | bytes 106528 | tf_op jit(solution)/shard_map/ppermute | solution.py:220
  28.8 0.7 %gradients.1 = (f32[256,128]{1,0:T(8,128)}, f32[128,128]{1,0:T(8,128)}, f32[8,128]{1,0:T(8,128)}, f32[4,128]{1,0:T(4,128)}) custom-call(f32[208,128]{1,0:T(8,128)S(1)} %convert_add_fusion.total, f32[208,128]{1,0:T(8,128)S(1)} %collective-permute-done.8.other), custom_call_target="tpu_custom_call" | custom-call | tf_op jit(solution)/shard_map/gradients/pallas_call | solution.py:392
  (3 shorter events, 0.1 us)
Async XLA Ops:
  3.7 6.8 %collective-permute-start.2 = (bf16[1,8,1024]{2,1,0:T(8,128)(2,1)S(1)}, bf16[1,8,1024]{2,1,0:T(8,128)(2,1)S(1)}, u32[]{:S(2)}, u32[]{:S(2)}) collective-permute-start(bf16[1,8,1024]{2,1,0:T(8,128)(2,1)S(1)} %bitcast.7), channel_id=1, source_target_pairs={{0,12},{1,13},{2,14},{3,15},{4,8},{5,9},{6,10},{7,11},{8,4},{9,5},... | collective-permute-start | bytes 49160 | tf_op jit(solution)/shard_map/ppermute | solution.py:220
  8.8 4.6 %collective-permute-start.1 = (bf16[1,8,1024]{2,1,0:T(8,128)(2,1)S(1)}, bf16[1,8,1024]{2,1,0:T(8,128)(2,1)S(1)}, u32[]{:S(2)}, u32[]{:S(2)}) collective-permute-start(bf16[1,8,1024]{2,1,0:T(8,128)(2,1)S(1)} %bitcast.8), channel_id=1, source_target_pairs={{0,8},{1,9},{2,10},{3,11},{4,12},{5,13},{6,14},{7,15},{8,0},{9,1},... | collective-permute-start | bytes 49160 | tf_op jit(solution)/shard_map/ppermute | solution.py:220
  8.8 4.6 %collective-permute-start = (bf16[1,8,1024]{2,1,0:T(8,128)(2,1)S(1)}, bf16[1,8,1024]{2,1,0:T(8,128)(2,1)S(1)}, u32[]{:S(2)}, u32[]{:S(2)}) collective-permute-start(bf16[1,8,1024]{2,1,0:T(8,128)(2,1)S(1)} %bitcast.9), channel_id=1, source_target_pairs={{0,4},{1,5},{2,6},{3,7},{4,0},{5,1},{6,2},{7,3},{8,12},{9,13},{10,... | collective-permute-start | bytes 49160 | tf_op jit(solution)/shard_map/ppermute | solution.py:220
  14.2 1.4 %collective-permute-start.3 = (f32[208,128]{1,0:T(8,128)S(1)}, f32[208,128]{1,0:T(8,128)S(1)}, u32[]{:S(2)}, u32[]{:S(2)}) collective-permute-start(f32[208,128]{1,0:T(8,128)S(1)} %get-tuple-element.54), channel_id=1, source_target_pairs={{0,1},{1,0},{2,3},{3,2},{4,5},{5,4},{6,7},{7,6},{8,9},{9,8},{10,11... | collective-permute-start | bytes 319496 | tf_op jit(solution)/shard_map/ppermute | solution.py:220
  15.6 5.4 %collective-permute-start.6 = (bf16[208,128]{1,0:T(8,128)(2,1)S(1)}, bf16[208,128]{1,0:T(8,128)(2,1)S(1)}, u32[]{:S(2)}, u32[]{:S(2)}) collective-permute-start(bf16[208,128]{1,0:T(8,128)(2,1)S(1)} %add_convert_fusion.1), channel_id=1, source_target_pairs={{0,6},{1,7},{2,4},{3,5},{4,2},{5,3},{6,0},{7,1},{8,14},{9,15},{10,... | collective-permute-start | bytes 159752 | tf_op jit(solution)/shard_map/ppermute | solution.py:220
  16.4 4.5 %collective-permute-start.5 = (bf16[208,128]{1,0:T(8,128)(2,1)S(1)}, bf16[208,128]{1,0:T(8,128)(2,1)S(1)}, u32[]{:S(2)}, u32[]{:S(2)}) collective-permute-start(bf16[208,128]{1,0:T(8,128)(2,1)S(1)} %add_convert_fusion.1), channel_id=1, source_target_pairs={{0,5},{1,4},{2,7},{3,6},{4,1},{5,0},{6,3},{7,2},{8,13},{9,12},{10,... | collective-permute-start | bytes 159752 | tf_op jit(solution)/shard_map/ppermute | solution.py:220
  18.1 3.6 %collective-permute-start.4 = (bf16[208,128]{1,0:T(8,128)(2,1)S(1)}, bf16[208,128]{1,0:T(8,128)(2,1)S(1)}, u32[]{:S(2)}, u32[]{:S(2)}) collective-permute-start(bf16[208,128]{1,0:T(8,128)(2,1)S(1)} %add_convert_fusion.1), channel_id=1, source_target_pairs={{0,3},{1,2},{2,1},{3,0},{4,7},{5,6},{6,5},{7,4},{8,11},{9,10},{10,... | collective-permute-start | bytes 159752 | tf_op jit(solution)/shard_map/ppermute | solution.py:220
  21.7 4.5 %collective-permute-start.7 = (bf16[208,128]{1,0:T(8,128)(2,1)S(1)}, bf16[208,128]{1,0:T(8,128)(2,1)S(1)}, u32[]{:S(2)}, u32[]{:S(2)}) collective-permute-start(bf16[208,128]{1,0:T(8,128)(2,1)S(1)} %add_convert_fusion), channel_id=1, source_target_pairs={{0,9},{1,8},{2,11},{3,10},{4,13},{5,12},{6,15},{7,14},{8,1},{9,0},... | collective-permute-start | bytes 159752 | tf_op jit(solution)/shard_map/ppermute | solution.py:220
  26.2 2.5 %collective-permute-start.8 = (f32[208,128]{1,0:T(8,128)S(1)}, f32[208,128]{1,0:T(8,128)S(1)}, u32[]{:S(2)}, u32[]{:S(2)}) collective-permute-start(f32[208,128]{1,0:T(8,128)S(1)} %convert_add_fusion.total), channel_id=1, source_target_pairs={{0,1},{1,0},{2,3},{3,2},{4,5},{5,4},{6,7},{7,6},{8,9},{9,8},{10,11... | collective-permute-start | bytes 319496 | tf_op jit(solution)/shard_map/ppermute | solution.py:220

commit v3 on v2

--- a/solution.py
+++ b/solution.py
@@ -13,7 +13,7 @@
 soft_square = 0.0625
 mesh_axes = ("member", "tile", "sample")
 row_block = 8
-point_chunk = 512
+point_chunk = 1024
 f32 = jnp.float32
 bf16 = jnp.bfloat16
 
@@ -179,8 +179,10 @@
         score[:, row, :] = value[:, row * cols : (row + 1) * cols]
 
 
-def output_kernel(total, other, grad_in, grad_mid, grad_out, grad_gains, sems):
+def output_kernel(total_in, other_in, grad_in, grad_mid, grad_out, grad_gains, total, other, sems):
     half = total.shape[0]
+    total[...] = total_in[...].astype(f32)
+    other[...] = other_in[...].astype(f32)
     moves = []
     first = 0
     for target in (grad_in, grad_mid, grad_out, grad_gains):
@@ -234,7 +236,7 @@
     parts = [block[None]]
     for bits in rounds_of(bits_of(lax.axis_size("member"), unit)):
         whole = parts[0] if len(parts) == 1 else jnp.concatenate(parts)
-        offsets = bits if len(bits) == 1 else [bits[0], bits[1], bits[0] ^ bits[1]]
+        offsets = bits if len(bits) == 1 else [bits[0], bits[0] ^ bits[1], bits[1]]
         parts = parts + [swap(whole, offset) for offset in offsets]
     return parts[1:]
 
@@ -242,28 +244,42 @@
 def reduction_bits():
     tiles, samples = lax.axis_size("tile"), lax.axis_size("sample")
     return bits_of(tiles, samples) + bits_of(lax.axis_size("member"), samples * tiles)
+
+
+def flipped():
+    return sum(reduction_bits())
+
+
+def crossing(offset):
+    return offset ^ (bin(offset & flipped()).count("1") & 1)
 
 
 def half_of_device():
     place = lax.axis_index(mesh_axes)
     which = place & 1
     for bit in reduction_bits():
-        which = which ^ jnp.where(place & bit, 1, 0)
+        if bit & flipped():
+            which = which ^ jnp.where(place & bit, 1, 0)
     return which
 
 
 def sum_parameters(keep, away, link_dtype):
-    total = keep + swap(away, 1)
+    total = keep + swap(away.astype(bf16), 1).astype(f32)
     for group in rounds_of(reduction_bits()):
         sent = total.astype(link_dtype)
         if len(group) == 1:
-            arrived = swap(sent, group[0] ^ 1)
+            arrived = swap(sent, crossing(group[0]))
             total = sent.astype(f32) + arrived.astype(f32)
         else:
             near, far = group
-            parts = [swap(sent, near ^ 1), swap(sent, far ^ 1), swap(sent, near ^ far)]
-            parts = [part.astype(f32) for part in parts]
-            total = (sent.astype(f32) + parts[0]) + (parts[1] + parts[2])
+            offsets = [near, far, near ^ far]
+            got = {}
+            for k in [0, 1, 2]:
+                got[k] = swap(sent, crossing(offsets[k]))
+
+            p = [got[k].astype(f32) for k in range(3)]
+            total = (sent.astype(f32) + p[0]) + (p[1] + p[2])
+    total = total.astype(bf16)
     return total, swap(total, 1)
 
 
@@ -395,7 +411,7 @@
         in_specs=[whole_spec(total), whole_spec(other)],
         out_specs=[pl.BlockSpec(memory_space=pltpu.HBM)] * 4,
         out_shape=shapes,
-        scratch_shapes=[pltpu.SemaphoreType.DMA((8,))],
+        scratch_shapes=[pltpu.VMEM(total.shape, f32)] * 2 + [pltpu.SemaphoreType.DMA((8,))],
         compiler_params=kernel_params,
         name="gradients",
     )(total, other)

time: 29.7 us -> 29.1 us (0.980)
  starting transfers between devices: 13 us -> 11 us
  waiting for transfers between devices: 9.65 us -> 11.4 us
  Pallas kernels: 5.44 us -> 5.14 us
    ppermute x9, starting transfers between devices: 13 us -> 11 us  [swap(): lax.ppermute(array, mesh_axes, [(place, place ^ offset) for place in rang...]
    ppermute x9, waiting for transfers between devices: 9.65 us -> 11.4 us  [swap(): lax.ppermute(array, mesh_axes, [(place, place ^ offset) for place in rang...]
    pallas_call x1, Pallas kernels: 2.37 us -> 2.06 us  [on_device(): pl.pallas_call(functools.partial(forward_kernel, chunk), grid=(steps,), i...]
  transfers between devices with their start and end apart: 9 -> 9, of which waited for: 7 -> 6; matrix products, arithmetic and copies ran while one was open for 0% -> 0% of each run, Pallas kernels for 5% -> 5%
where the time goes in v3:
time: 29.1 us; the launch traced here: 29 us
  waiting for transfers between devices  11.4 us (39%)
  starting transfers between devices  11 us (38%)
  Pallas kernels  5.14 us (18%)
  between operations  1.34 us (5%)
    ppermute x9, waiting for transfers between devices, swap(): lax.ppermute(array, mesh_axes, [(place, place ^ offset) for place in rang...  11.4 us
    ppermute x9, starting transfers between devices, swap(): lax.ppermute(array, mesh_axes, [(place, place ^ offset) for place in rang...  11 us
    pallas_call x1, Pallas kernels, on_device(): pl.pallas_call(functools.partial(forward_kernel, chunk), grid=(steps,), i...  2.06 us
    pallas_call x1, Pallas kernels, on_device(): pl.pallas_call(derivative_kernel, grid=(steps,), in_specs=[by_point((poin...  0.94 us
    pallas_call x1, Pallas kernels, on_device(): pl.pallas_call(output_kernel, grid=(1,), in_specs=[whole_spec(total), who...  0.76 us
    pallas_call x1, Pallas kernels, on_device(): pl.pallas_call(functools.partial(backward_kernel, steps, norm_factor / me...  0.74 us
    pallas_call x1, Pallas kernels, on_device(): pl.pallas_call(functools.partial(score_kernel, len(parts)), grid=(1,), in...  0.64 us
  transfers between devices with their start and end apart: 9, of which 6 were waited for; matrix products, arithmetic and copies ran while one was open for 0% of the time, Pallas kernels for 5%

profile of v3, /device:TPU:0, one launch (start us, length us, event | category | flops | bytes accessed | tf_op | source)
XLA Modules:
  0.0 29.0 jit_solution(13565167910129218563)
XLA Ops:
  1.3 2.1 %forward.1 = (bf16[1024,256]{1,0:T(8,128)(2,1)S(1)}, f32[8,4,256]{2,1,0:T(4,128)S(1)}, s32[4,256]{1,0:T(4,128)S(1)}, f32[1024,128]{1,0:T(8,128)S(1)}, f32[1024,1...) custom-call(s32[1,1]{1,0:T(1,128)S(6)} %copy.13.order, ...), custom_call_target="tpu_custom_call" | custom-call | tf_op jit(solution)/shard_map/forward/pallas_call | solution.py:330
  3.3 4.1 %collective-permute-start.2 = (bf16[1,8,1024]{2,1,0:T(8,128)(2,1)S(1)}, bf16[1,8,1024]{2,1,0:T(8,128)(2,1)S(1)}, u32[]{:S(2)}, u32[]{:S(2)}) collective-permute-start(bf16[1,8,1024]{2,1,0:T(8,128)(2,1)S(1)} %bitcast.7), channel_id=1, source_target_pairs={{0,8},{1,9},{2,10},{3,11},{4,12},{5,13},{6,14},{7,15},{8,0},{9,1},... | collective-permute-start | bytes 49160 | tf_op jit(solution)/shard_map/ppermute | solution.py:222
  7.4 1.3 %collective-permute-start.1 = (bf16[1,8,1024]{2,1,0:T(8,128)(2,1)S(1)}, bf16[1,8,1024]{2,1,0:T(8,128)(2,1)S(1)}, u32[]{:S(2)}, u32[]{:S(2)}) collective-permute-start(bf16[1,8,1024]{2,1,0:T(8,128)(2,1)S(1)} %bitcast.8), channel_id=1, source_target_pairs={{0,12},{1,13},{2,14},{3,15},{4,8},{5,9},{6,10},{7,11},{8,4},{9,5},... | collective-permute-start | bytes 49160 | tf_op jit(solution)/shard_map/ppermute | solution.py:222
  8.8 0.2 collective-permute-start
  9.0 0.9 %derivatives.1 = (f32[1024,128]{1,0:T(8,128)S(1)}, f32[1024,128]{1,0:T(8,128)S(1)}, f32[1024,128]{1,0:T(8,128)S(1)}, bf16[256,1024]{1,0:T(8,128)(2,1)S(1)}, bf16...) custom-call(bf16[1024,256]{1,0:T(8,128)(2,1)S(1)} %get-tuple-element.33.latent, ...), custom_call_target="tpu_custom_call" | custom-call | tf_op jit(solution)/shard_map/derivatives/pallas_call | solution.py:356
  10.0 0.0 collective-permute-done.2.refs_2_.refs_5_
  10.0 3.0 %collective-permute-done.1.refs_1_.refs_4_ = bf16[1,8,1024]{2,1,0:T(8,128)(2,1)S(1)} collective-permute-done((bf16[1,8,1024]{2,1,0:T(8,128)(2,1)S(1)}, bf16[1,8,1024]{2,1,0:T(8,128)(2,1)S(1)}, u32[]{:S(2)}, u32[]{:S(2)}) %collective-permute-start.1) | collective-permute-done | bytes 16416 | tf_op jit(solution)/shard_map/ppermute | solution.py:222
  13.0 0.0 collective-permute-done.refs_0_.refs_3_
  13.0 0.7 %backward.1 = (f32[208,128]{1,0:T(8,128)S(1)}, f32[208,128]{1,0:T(8,128)S(1)}) custom-call(s32[1,1]{1,0:T(1,128)S(6)} %copy.13.order, f32[8,1024]{1,0:T(8,128)S(1)} %get-tuple-element.32.predicted.refs_0_, f32[8,1024]{1,0:T(8,128)S(1)} %get-tuple-element.42.target.refs_1_, f32[1,1024]{1,0:T(1,128)S(1)} %get-tuple-element.43.valid.refs_2_, ...), custom_call_target="tpu_custom_call" | custom-call | tf_op jit(solution)/shard_map/backward/pallas_call | solution.py:370
  13.8 0.1 collective-permute-start.3
  13.8 1.2 %collective-permute-done.3 = bf16[208,128]{1,0:T(8,128)(2,1)S(1)} collective-permute-done((bf16[208,128]{1,0:T(8,128)(2,1)S(1)}, bf16[208,128]{1,0:T(8,128)(2,1)S(1)}, u32[]{:S(2)}, u32[]{:S(2)}) %collective-permute-start.3) | collective-permute-done | bytes 53280 | tf_op jit(solution)/shard_map/ppermute | solution.py:222
  15.1 0.8 %collective-permute-start.6 = (bf16[208,128]{1,0:T(8,128)(2,1)S(1)}, bf16[208,128]{1,0:T(8,128)(2,1)S(1)}, u32[]{:S(2)}, u32[]{:S(2)}) collective-permute-start(bf16[208,128]{1,0:T(8,128)(2,1)S(1)} %add_convert_fusion.2), channel_id=1, source_target_pairs={{0,6},{1,7},{2,4},{3,5},{4,2},{5,3},{6,0},{7,1},{8,14},{9,15},{10,... | collective-permute-start | bytes 159752 | tf_op jit(solution)/shard_map/ppermute | solution.py:222
  15.8 1.7 %collective-permute-start.5 = (bf16[208,128]{1,0:T(8,128)(2,1)S(1)}, bf16[208,128]{1,0:T(8,128)(2,1)S(1)}, u32[]{:S(2)}, u32[]{:S(2)}) collective-permute-start(bf16[208,128]{1,0:T(8,128)(2,1)S(1)} %add_convert_fusion.2), channel_id=1, source_target_pairs={{0,5},{1,4},{2,7},{3,6},{4,1},{5,0},{6,3},{7,2},{8,13},{9,12},{10,... | collective-permute-start | bytes 159752 | tf_op jit(solution)/shard_map/ppermute | solution.py:222
  17.6 0.8 %collective-permute-start.4 = (bf16[208,128]{1,0:T(8,128)(2,1)S(1)}, bf16[208,128]{1,0:T(8,128)(2,1)S(1)}, u32[]{:S(2)}, u32[]{:S(2)}) collective-permute-start(bf16[208,128]{1,0:T(8,128)(2,1)S(1)} %add_convert_fusion.2), channel_id=1, source_target_pairs={{0,3},{1,2},{2,1},{3,0},{4,7},{5,6},{6,5},{7,4},{8,11},{9,10},{10,... | collective-permute-start | bytes 159752 | tf_op jit(solution)/shard_map/ppermute | solution.py:222
  18.4 2.2 %collective-permute-done.6 = bf16[208,128]{1,0:T(8,128)(2,1)S(1)} collective-permute-done((bf16[208,128]{1,0:T(8,128)(2,1)S(1)}, bf16[208,128]{1,0:T(8,128)(2,1)S(1)}, u32[]{:S(2)}, u32[]{:S(2)}) %collective-permute-start.6) | collective-permute-done | bytes 53280 | tf_op jit(solution)/shard_map/ppermute | solution.py:222
  20.5 0.0 collective-permute-done.5
  20.5 0.6 %collective-permute-done.4 = bf16[208,128]{1,0:T(8,128)(2,1)S(1)} collective-permute-done((bf16[208,128]{1,0:T(8,128)(2,1)S(1)}, bf16[208,128]{1,0:T(8,128)(2,1)S(1)}, u32[]{:S(2)}, u32[]{:S(2)}) %collective-permute-start.4) | collective-permute-done | bytes 53280 | tf_op jit(solution)/shard_map/ppermute | solution.py:222
  21.2 1.5 %collective-permute-start.7 = (bf16[208,128]{1,0:T(8,128)(2,1)S(1)}, bf16[208,128]{1,0:T(8,128)(2,1)S(1)}, u32[]{:S(2)}, u32[]{:S(2)}) collective-permute-start(bf16[208,128]{1,0:T(8,128)(2,1)S(1)} %add_convert_fusion.1), channel_id=1, source_target_pairs={{0,9},{1,8},{2,11},{3,10},{4,13},{5,12},{6,15},{7,14},{8,1},{9,0},... | collective-permute-start | bytes 159752 | tf_op jit(solution)/shard_map/ppermute | solution.py:222
  22.7 4.2 %collective-permute-done.7 = bf16[208,128]{1,0:T(8,128)(2,1)S(1)} collective-permute-done((bf16[208,128]{1,0:T(8,128)(2,1)S(1)}, bf16[208,128]{1,0:T(8,128)(2,1)S(1)}, u32[]{:S(2)}, u32[]{:S(2)}) %collective-permute-start.7) | collective-permute-done | bytes 53280 | tf_op jit(solution)/shard_map/ppermute | solution.py:222
  26.9 0.4 %collective-permute-start.8 = (bf16[208,128]{1,0:T(8,128)(2,1)S(1)}, bf16[208,128]{1,0:T(8,128)(2,1)S(1)}, u32[]{:S(2)}, u32[]{:S(2)}) collective-permute-start(bf16[208,128]{1,0:T(8,128)(2,1)S(1)} %add_convert_fusion.total_in), channel_id=1, source_target_pairs={{0,1},{1,0},{2,3},{3,2},{4,5},{5,4},{6,7},{7,6},{8,9},{9,8},{10,11... | collective-permute-start | bytes 159752 | tf_op jit(solution)/shard_map/ppermute | solution.py:222
  27.3 0.6 %score.1 = f32[8,1,256]{2,1,0:T(1,128)} custom-call(f32[8,1024]{1,0:T(8,128)S(1)} %get-tuple-element.32.predicted.refs_0_, f32[8,1024]{1,0:T(8,128)S(1)} %get-tuple-element.42.target.refs_1_, f32[1,1024]{1,0:T(1,128)S(1)} %get-tuple-element.43.valid.refs_2_, bf16[1,8,1024]{2,1,0:T(8,128)(2,1)S(1)} %collective-permute-done.refs_0_.refs_3_, ...), custom_call_target="tpu_custom_call" | custom-call | tf_op jit(solution)/shard_map/score/pallas_call | solution.py:396
  28.0 0.2 collective-permute-done.8.other_in
  28.2 0.8 %gradients.1 = (f32[256,128]{1,0:T(8,128)}, f32[128,128]{1,0:T(8,128)}, f32[8,128]{1,0:T(8,128)}, f32[4,128]{1,0:T(4,128)}) custom-call(bf16[208,128]{1,0:T(8,128)(2,1)S(1)} %add_convert_fusion.total_in, bf16[208,128]{1,0:T(8,128)(2,1)S(1)} %collective-permute-done.8.other_in), custom_call_target="tpu_custom_call" | custom-call | tf_op jit(solution)/shard_map/gradients/pallas_call | solution.py:408
  (4 shorter events, 0.1 us)
Async XLA Ops:
  3.3 6.6 %collective-permute-start.2 = (bf16[1,8,1024]{2,1,0:T(8,128)(2,1)S(1)}, bf16[1,8,1024]{2,1,0:T(8,128)(2,1)S(1)}, u32[]{:S(2)}, u32[]{:S(2)}) collective-permute-start(bf16[1,8,1024]{2,1,0:T(8,128)(2,1)S(1)} %bitcast.7), channel_id=1, source_target_pairs={{0,8},{1,9},{2,10},{3,11},{4,12},{5,13},{6,14},{7,15},{8,0},{9,1},... | collective-permute-start | bytes 49160 | tf_op jit(solution)/shard_map/ppermute | solution.py:222
  7.4 5.5 %collective-permute-start.1 = (bf16[1,8,1024]{2,1,0:T(8,128)(2,1)S(1)}, bf16[1,8,1024]{2,1,0:T(8,128)(2,1)S(1)}, u32[]{:S(2)}, u32[]{:S(2)}) collective-permute-start(bf16[1,8,1024]{2,1,0:T(8,128)(2,1)S(1)} %bitcast.8), channel_id=1, source_target_pairs={{0,12},{1,13},{2,14},{3,15},{4,8},{5,9},{6,10},{7,11},{8,4},{9,5},... | collective-permute-start | bytes 49160 | tf_op jit(solution)/shard_map/ppermute | solution.py:222
  8.8 4.2 %collective-permute-start = (bf16[1,8,1024]{2,1,0:T(8,128)(2,1)S(1)}, bf16[1,8,1024]{2,1,0:T(8,128)(2,1)S(1)}, u32[]{:S(2)}, u32[]{:S(2)}) collective-permute-start(bf16[1,8,1024]{2,1,0:T(8,128)(2,1)S(1)} %bitcast.9), channel_id=1, source_target_pairs={{0,4},{1,5},{2,6},{3,7},{4,0},{5,1},{6,2},{7,3},{8,12},{9,13},{10,... | collective-permute-start | bytes 49160 | tf_op jit(solution)/shard_map/ppermute | solution.py:222
  13.8 1.3 %collective-permute-start.3 = (bf16[208,128]{1,0:T(8,128)(2,1)S(1)}, bf16[208,128]{1,0:T(8,128)(2,1)S(1)}, u32[]{:S(2)}, u32[]{:S(2)}) collective-permute-start(bf16[208,128]{1,0:T(8,128)(2,1)S(1)} %convert_element_type.33), channel_id=1, source_target_pairs={{0,1},{1,0},{2,3},{3,2},{4,5},{5,4},{6,7},{7,6},{8,9},{9,8},{10,11... | collective-permute-start | bytes 159752 | tf_op jit(solution)/shard_map/ppermute | solution.py:222
  15.1 5.4 %collective-permute-start.6 = (bf16[208,128]{1,0:T(8,128)(2,1)S(1)}, bf16[208,128]{1,0:T(8,128)(2,1)S(1)}, u32[]{:S(2)}, u32[]{:S(2)}) collective-permute-start(bf16[208,128]{1,0:T(8,128)(2,1)S(1)} %add_convert_fusion.2), channel_id=1, source_target_pairs={{0,6},{1,7},{2,4},{3,5},{4,2},{5,3},{6,0},{7,1},{8,14},{9,15},{10,... | collective-permute-start | bytes 159752 | tf_op jit(solution)/shard_map/ppermute | solution.py:222
  15.8 4.7 %collective-permute-start.5 = (bf16[208,128]{1,0:T(8,128)(2,1)S(1)}, bf16[208,128]{1,0:T(8,128)(2,1)S(1)}, u32[]{:S(2)}, u32[]{:S(2)}) collective-permute-start(bf16[208,128]{1,0:T(8,128)(2,1)S(1)} %add_convert_fusion.2), channel_id=1, source_target_pairs={{0,5},{1,4},{2,7},{3,6},{4,1},{5,0},{6,3},{7,2},{8,13},{9,12},{10,... | collective-permute-start | bytes 159752 | tf_op jit(solution)/shard_map/ppermute | solution.py:222
  17.6 3.6 %collective-permute-start.4 = (bf16[208,128]{1,0:T(8,128)(2,1)S(1)}, bf16[208,128]{1,0:T(8,128)(2,1)S(1)}, u32[]{:S(2)}, u32[]{:S(2)}) collective-permute-start(bf16[208,128]{1,0:T(8,128)(2,1)S(1)} %add_convert_fusion.2), channel_id=1, source_target_pairs={{0,3},{1,2},{2,1},{3,0},{4,7},{5,6},{6,5},{7,4},{8,11},{9,10},{10,... | collective-permute-start | bytes 159752 | tf_op jit(solution)/shard_map/ppermute | solution.py:222
  21.2 5.7 %collective-permute-start.7 = (bf16[208,128]{1,0:T(8,128)(2,1)S(1)}, bf16[208,128]{1,0:T(8,128)(2,1)S(1)}, u32[]{:S(2)}, u32[]{:S(2)}) collective-permute-start(bf16[208,128]{1,0:T(8,128)(2,1)S(1)} %add_convert_fusion.1), channel_id=1, source_target_pairs={{0,9},{1,8},{2,11},{3,10},{4,13},{5,12},{6,15},{7,14},{8,1},{9,0},... | collective-permute-start | bytes 159752 | tf_op jit(solution)/shard_map/ppermute | solution.py:222
  26.9 1.3 %collective-permute-start.8 = (bf16[208,128]{1,0:T(8,128)(2,1)S(1)}, bf16[208,128]{1,0:T(8,128)(2,1)S(1)}, u32[]{:S(2)}, u32[]{:S(2)}) collective-permute-start(bf16[208,128]{1,0:T(8,128)(2,1)S(1)} %add_convert_fusion.total_in), channel_id=1, source_target_pairs={{0,1},{1,0},{2,3},{3,2},{4,5},{5,4},{6,7},{7,6},{8,9},{9,8},{10,11... | collective-permute-start | bytes 159752 | tf_op jit(solution)/shard_map/ppermute | solution.py:222

commit v4 on v2

--- a/solution.py
+++ b/solution.py
@@ -13,7 +13,7 @@
 soft_square = 0.0625
 mesh_axes = ("member", "tile", "sample")
 row_block = 8
-point_chunk = 512
+point_chunk = 1024
 f32 = jnp.float32
 bf16 = jnp.bfloat16
 
@@ -230,40 +230,66 @@
 
 
 def gather_members(block):
+    members = lax.axis_size("member")
+    if members == 4:
+        routes = [(1, 0, 3, 2), (3, 2, 0, 1), (2, 3, 1, 0)]
+        return [lax.ppermute(block[None], "member", list(enumerate(route))) for route in routes]
     unit = lax.axis_size("tile") * lax.axis_size("sample")
     parts = [block[None]]
-    for bits in rounds_of(bits_of(lax.axis_size("member"), unit)):
+    for bits in rounds_of(bits_of(members, unit)):
         whole = parts[0] if len(parts) == 1 else jnp.concatenate(parts)
         offsets = bits if len(bits) == 1 else [bits[0], bits[1], bits[0] ^ bits[1]]
         parts = parts + [swap(whole, offset) for offset in offsets]
     return parts[1:]
 
 
-def reduction_bits():
-    tiles, samples = lax.axis_size("tile"), lax.axis_size("sample")
-    return bits_of(tiles, samples) + bits_of(lax.axis_size("member"), samples * tiles)
+def chip_bits():
+    tiles = lax.axis_size("tile")
+    return bits_of(tiles, 1), bits_of(lax.axis_size("member"), tiles)
+
+
+def turned(chip, chips):
+    if chips == 8:
+        return (41 >> chip) & 1
+    value = 0
+    for place in range(chips.bit_length() - 1):
+        value = value ^ ((chip >> place) & 1)
+    return value
 
 
 def half_of_device():
     place = lax.axis_index(mesh_axes)
-    which = place & 1
-    for bit in reduction_bits():
-        which = which ^ jnp.where(place & bit, 1, 0)
-    return which
+    return (place & 1) ^ turned(place >> 1, lax.axis_size("member") * lax.axis_size("tile"))
+
+
+def cross(array, partner):
+    chips = lax.axis_size("member") * lax.axis_size("tile")
+    pairs = []
+    for chip in range(chips):
+        other = partner(chip)
+        turn = turned(chip, chips) ^ turned(other, chips)
+        pairs += [(2 * chip + core, 2 * other + (core ^ turn)) for core in range(2)]
+    return lax.ppermute(array, mesh_axes, pairs)
 
 
 def sum_parameters(keep, away, link_dtype):
-    total = keep + swap(away, 1)
-    for group in rounds_of(reduction_bits()):
+    assert lax.axis_size("sample") == 2
+    sent = (keep + swap(away, 1)).astype(link_dtype)
+    tile_bits, member_bits = chip_bits()
+    groups = rounds_of(tile_bits + member_bits)
+    for place, group in enumerate(groups):
+        if len(group) == 2:
+            near, far = group
+            one, two, three = (
+                cross(sent, lambda chip: chip ^ offset).astype(f32) for offset in (near, far, near ^ far)
+            )
+            total = (sent.astype(f32) + one) + (two + three)
+        else:
+            turn = tile_bits[0] if place == len(groups) - 1 and place > 0 else 0
+            odd = member_bits[0]
+            arrived = cross(sent, lambda chip: chip ^ group[0] ^ (turn if chip & odd else 0))
+            total = sent.astype(f32) + arrived.astype(f32)
         sent = total.astype(link_dtype)
-        if len(group) == 1:
-            arrived = swap(sent, group[0] ^ 1)
-            total = sent.astype(f32) + arrived.astype(f32)
-        else:
-            near, far = group
-            parts = [swap(sent, near ^ 1), swap(sent, far ^ 1), swap(sent, near ^ far)]
-            parts = [part.astype(f32) for part in parts]
-            total = (sent.astype(f32) + parts[0]) + (parts[1] + parts[2])
     return total, swap(total, 1)
 
 

time: 29.7 us -> 27.9 us (0.939)
  starting transfers between devices: 13 us -> 11.2 us
  Pallas kernels: 5.44 us -> 5.13 us
    ppermute x9 -> x2, starting transfers between devices: 13 us -> 0.43 us  [swap(): lax.ppermute(array, mesh_axes, [(place, place ^ offset) for place in rang...]
    ppermute x0 -> x7, starting transfers between devices: none -> 10.8 us  [the longest x3 5.67 us: gather_members(): lax.ppermute(block[None], 'member', list(enumerate(route)))]
    ppermute x0 -> x7, waiting for transfers between devices: none -> 8.26 us  [the longest x4 5.97 us: cross(): return lax.ppermute(array, mesh_axes, pairs)]
    ppermute x9 -> x2, waiting for transfers between devices: 9.65 us -> 1.67 us  [swap(): lax.ppermute(array, mesh_axes, [(place, place ^ offset) for place in rang...]
    pallas_call x1, Pallas kernels: 2.37 us -> 2.06 us  [on_device(): pl.pallas_call(functools.partial(forward_kernel, chunk), grid=(steps,), i...]
  transfers between devices with their start and end apart: 9 -> 9, of which waited for: 7 -> 8; matrix products, arithmetic and copies ran while one was open for 0% -> 0% of each run, Pallas kernels for 5% -> 6%
where the time goes in v4:
time: 27.9 us; the launch traced here: 27.7 us
  starting transfers between devices  11.2 us (40%)
  waiting for transfers between devices  9.93 us (36%)
  Pallas kernels  5.13 us (18%)
  between operations  1.33 us (5%)
    ppermute x4, waiting for transfers between devices, cross(): return lax.ppermute(array, mesh_axes, pairs)  5.97 us
    ppermute x3, starting transfers between devices, gather_members(): lax.ppermute(block[None], 'member', list(enumerate(route)))  5.67 us
    ppermute x4, starting transfers between devices, cross(): return lax.ppermute(array, mesh_axes, pairs)  5.13 us
    ppermute x3, waiting for transfers between devices, gather_members(): lax.ppermute(block[None], 'member', list(enumerate(route)))  2.29 us
    pallas_call x1, Pallas kernels, on_device(): pl.pallas_call(functools.partial(forward_kernel, chunk), grid=(steps,), i...  2.06 us
    ppermute x2, waiting for transfers between devices, swap(): lax.ppermute(array, mesh_axes, [(place, place ^ offset) for place in rang...  1.67 us
    pallas_call x1, Pallas kernels, on_device(): pl.pallas_call(derivative_kernel, grid=(steps,), in_specs=[by_point((poin...  0.94 us
    pallas_call x1, Pallas kernels, on_device(): pl.pallas_call(output_kernel, grid=(1,), in_specs=[whole_spec(total), who...  0.75 us
  transfers between devices with their start and end apart: 9, of which 8 were waited for; matrix products, arithmetic and copies ran while one was open for 0% of the time, Pallas kernels for 6%

profile of v4, /device:TPU:0, one launch (start us, length us, event | category | flops | bytes accessed | tf_op | source)
XLA Modules:
  0.0 27.7 jit_solution(3025652296372267470)
XLA Ops:
  1.3 2.1 %forward.1 = (bf16[1024,256]{1,0:T(8,128)(2,1)S(1)}, f32[8,4,256]{2,1,0:T(4,128)S(1)}, s32[4,256]{1,0:T(4,128)S(1)}, f32[1024,128]{1,0:T(8,128)S(1)}, f32[1024,1...) custom-call(s32[1,1]{1,0:T(1,128)S(6)} %copy.13.order, ...), custom_call_target="tpu_custom_call" | custom-call | tf_op jit(solution)/shard_map/forward/pallas_call | solution.py:340
  3.3 4.1 %collective-permute-start.2 = (bf16[1,8,1024]{2,1,0:T(8,128)(2,1)S(1)}, bf16[1,8,1024]{2,1,0:T(8,128)(2,1)S(1)}, u32[]{:S(2)}, u32[]{:S(2)}) collective-permute-start(bf16[1,8,1024]{2,1,0:T(8,128)(2,1)S(1)} %bitcast.7), channel_id=1, source_target_pairs={{0,8},{4,12},{8,4},{12,0},{1,9},{5,13},{9,5},{13,1},{2,10},{6,14},... | collective-permute-start | bytes 49160 | tf_op jit(solution)/shard_map/ppermute | solution.py:236
  7.4 1.1 %collective-permute-start.1 = (bf16[1,8,1024]{2,1,0:T(8,128)(2,1)S(1)}, bf16[1,8,1024]{2,1,0:T(8,128)(2,1)S(1)}, u32[]{:S(2)}, u32[]{:S(2)}) collective-permute-start(bf16[1,8,1024]{2,1,0:T(8,128)(2,1)S(1)} %bitcast.8), channel_id=1, source_target_pairs={{0,12},{4,8},{8,0},{12,4},{1,13},{5,9},{9,1},{13,5},{2,14},{6,10},... | collective-permute-start | bytes 49160 | tf_op jit(solution)/shard_map/ppermute | solution.py:236
  8.5 0.5 %collective-permute-start = (bf16[1,8,1024]{2,1,0:T(8,128)(2,1)S(1)}, bf16[1,8,1024]{2,1,0:T(8,128)(2,1)S(1)}, u32[]{:S(2)}, u32[]{:S(2)}) collective-permute-start(bf16[1,8,1024]{2,1,0:T(8,128)(2,1)S(1)} %bitcast.9), channel_id=1, source_target_pairs={{0,4},{4,0},{8,12},{12,8},{1,5},{5,1},{9,13},{13,9},{2,6},{6,2},{1... | collective-permute-start | bytes 49160 | tf_op jit(solution)/shard_map/ppermute | solution.py:236
  9.0 0.9 %derivatives.1 = (f32[1024,128]{1,0:T(8,128)S(1)}, f32[1024,128]{1,0:T(8,128)S(1)}, f32[1024,128]{1,0:T(8,128)S(1)}, bf16[256,1024]{1,0:T(8,128)(2,1)S(1)}, bf16...) custom-call(bf16[1024,256]{1,0:T(8,128)(2,1)S(1)} %get-tuple-element.33.latent, ...), custom_call_target="tpu_custom_call" | custom-call | tf_op jit(solution)/shard_map/derivatives/pallas_call | solution.py:366
  10.0 0.2 collective-permute-done.2.refs_2_.refs_5_
  10.2 1.9 %collective-permute-done.1.refs_1_.refs_4_ = bf16[1,8,1024]{2,1,0:T(8,128)(2,1)S(1)} collective-permute-done((bf16[1,8,1024]{2,1,0:T(8,128)(2,1)S(1)}, bf16[1,8,1024]{2,1,0:T(8,128)(2,1)S(1)}, u32[]{:S(2)}, u32[]{:S(2)}) %collective-permute-start.1) | collective-permute-done | bytes 16416 | tf_op jit(solution)/shard_map/ppermute | solution.py:236
  12.1 0.2 collective-permute-done.refs_0_.refs_3_
  12.2 0.7 %backward.1 = (f32[208,128]{1,0:T(8,128)S(1)}, f32[208,128]{1,0:T(8,128)S(1)}) custom-call(s32[1,1]{1,0:T(1,128)S(6)} %copy.13.order, f32[8,1024]{1,0:T(8,128)S(1)} %get-tuple-element.32.predicted.refs_0_, f32[8,1024]{1,0:T(8,128)S(1)} %get-tuple-element.42.target.refs_1_, f32[1,1024]{1,0:T(1,128)S(1)} %get-tuple-element.43.valid.refs_2_, ...), custom_call_target="tpu_custom_call" | custom-call | tf_op jit(solution)/shard_map/backward/pallas_call | solution.py:380
  13.0 0.1 collective-permute-start.3
  13.1 1.3 %collective-permute-done.3 = f32[208,128]{1,0:T(8,128)S(1)} collective-permute-done((f32[208,128]{1,0:T(8,128)S(1)}, f32[208,128]{1,0:T(8,128)S(1)}, u32[]{:S(2)}, u32[]{:S(2)}) %collective-permute-start.3) | collective-permute-done | bytes 106528 | tf_op jit(solution)/shard_map/ppermute | solution.py:220
  14.4 2.4 %collective-permute-start.6 = (bf16[208,128]{1,0:T(8,128)(2,1)S(1)}, bf16[208,128]{1,0:T(8,128)(2,1)S(1)}, u32[]{:S(2)}, u32[]{:S(2)}) collective-permute-start(bf16[208,128]{1,0:T(8,128)(2,1)S(1)} %add_convert_fusion.1), channel_id=1, source_target_pairs={{0,6},{1,7},{2,4},{3,5},{4,2},{5,3},{6,0},{7,1},{8,14},{9,15},{10,... | collective-permute-start | bytes 159752 | tf_op jit(solution)/shard_map/ppermute | solution.py:272
  16.8 0.3 collective-permute-start.5
  17.0 0.6 %collective-permute-start.4 = (bf16[208,128]{1,0:T(8,128)(2,1)S(1)}, bf16[208,128]{1,0:T(8,128)(2,1)S(1)}, u32[]{:S(2)}, u32[]{:S(2)}) collective-permute-start(bf16[208,128]{1,0:T(8,128)(2,1)S(1)} %add_convert_fusion.1), channel_id=1, source_target_pairs={{0,3},{1,2},{2,1},{3,0},{4,7},{5,6},{6,5},{7,4},{8,11},{9,10},{10,... | collective-permute-start | bytes 159752 | tf_op jit(solution)/shard_map/ppermute | solution.py:272
  17.7 1.8 %collective-permute-done.6 = bf16[208,128]{1,0:T(8,128)(2,1)S(1)} collective-permute-done((bf16[208,128]{1,0:T(8,128)(2,1)S(1)}, bf16[208,128]{1,0:T(8,128)(2,1)S(1)}, u32[]{:S(2)}, u32[]{:S(2)}) %collective-permute-start.6) | collective-permute-done | bytes 53280 | tf_op jit(solution)/shard_map/ppermute | solution.py:272
  19.5 1.4 %collective-permute-done.5 = bf16[208,128]{1,0:T(8,128)(2,1)S(1)} collective-permute-done((bf16[208,128]{1,0:T(8,128)(2,1)S(1)}, bf16[208,128]{1,0:T(8,128)(2,1)S(1)}, u32[]{:S(2)}, u32[]{:S(2)}) %collective-permute-start.5) | collective-permute-done | bytes 53280 | tf_op jit(solution)/shard_map/ppermute | solution.py:272
  20.9 0.0 collective-permute-done.4
  20.9 1.9 %collective-permute-start.7 = (bf16[208,128]{1,0:T(8,128)(2,1)S(1)}, bf16[208,128]{1,0:T(8,128)(2,1)S(1)}, u32[]{:S(2)}, u32[]{:S(2)}) collective-permute-start(bf16[208,128]{1,0:T(8,128)(2,1)S(1)} %add_convert_fusion), channel_id=1, source_target_pairs={{0,9},{1,8},{2,11},{3,10},{4,14},{5,15},{6,13},{7,12},{8,1},{9,0},... | collective-permute-start | bytes 159752 | tf_op jit(solution)/shard_map/ppermute | solution.py:272
  22.8 2.8 %collective-permute-done.7 = bf16[208,128]{1,0:T(8,128)(2,1)S(1)} collective-permute-done((bf16[208,128]{1,0:T(8,128)(2,1)S(1)}, bf16[208,128]{1,0:T(8,128)(2,1)S(1)}, u32[]{:S(2)}, u32[]{:S(2)}) %collective-permute-start.7) | collective-permute-done | bytes 53280 | tf_op jit(solution)/shard_map/ppermute | solution.py:272
  25.6 0.4 %collective-permute-start.8 = (f32[208,128]{1,0:T(8,128)S(1)}, f32[208,128]{1,0:T(8,128)S(1)}, u32[]{:S(2)}, u32[]{:S(2)}) collective-permute-start(f32[208,128]{1,0:T(8,128)S(1)} %convert_add_fusion.total), channel_id=1, source_target_pairs={{0,1},{1,0},{2,3},{3,2},{4,5},{5,4},{6,7},{7,6},{8,9},{9,8},{10,11... | collective-permute-start | bytes 319496 | tf_op jit(solution)/shard_map/ppermute | solution.py:220
  25.9 0.6 %score.1 = f32[8,1,256]{2,1,0:T(1,128)} custom-call(f32[8,1024]{1,0:T(8,128)S(1)} %get-tuple-element.32.predicted.refs_0_, f32[8,1024]{1,0:T(8,128)S(1)} %get-tuple-element.42.target.refs_1_, f32[1,1024]{1,0:T(1,128)S(1)} %get-tuple-element.43.valid.refs_2_, bf16[1,8,1024]{2,1,0:T(8,128)(2,1)S(1)} %collective-permute-done.refs_0_.refs_3_, ...), custom_call_target="tpu_custom_call" | custom-call | tf_op jit(solution)/shard_map/score/pallas_call | solution.py:406
  26.6 0.4 %collective-permute-done.8.other = f32[208,128]{1,0:T(8,128)S(1)} collective-permute-done((f32[208,128]{1,0:T(8,128)S(1)}, f32[208,128]{1,0:T(8,128)S(1)}, u32[]{:S(2)}, u32[]{:S(2)}) %collective-permute-start.8) | collective-permute-done | bytes 106528 | tf_op jit(solution)/shard_map/ppermute | solution.py:220
  26.9 0.7 %gradients.1 = (f32[256,128]{1,0:T(8,128)}, f32[128,128]{1,0:T(8,128)}, f32[8,128]{1,0:T(8,128)}, f32[4,128]{1,0:T(4,128)}) custom-call(f32[208,128]{1,0:T(8,128)S(1)} %convert_add_fusion.total, f32[208,128]{1,0:T(8,128)S(1)} %collective-permute-done.8.other), custom_call_target="tpu_custom_call" | custom-call | tf_op jit(solution)/shard_map/gradients/pallas_call | solution.py:418
  (3 shorter events, 0.1 us)
Async XLA Ops:
  3.3 6.8 %collective-permute-start.2 = (bf16[1,8,1024]{2,1,0:T(8,128)(2,1)S(1)}, bf16[1,8,1024]{2,1,0:T(8,128)(2,1)S(1)}, u32[]{:S(2)}, u32[]{:S(2)}) collective-permute-start(bf16[1,8,1024]{2,1,0:T(8,128)(2,1)S(1)} %bitcast.7), channel_id=1, source_target_pairs={{0,8},{4,12},{8,4},{12,0},{1,9},{5,13},{9,5},{13,1},{2,10},{6,14},... | collective-permute-start | bytes 49160 | tf_op jit(solution)/shard_map/ppermute | solution.py:236
  7.4 4.6 %collective-permute-start.1 = (bf16[1,8,1024]{2,1,0:T(8,128)(2,1)S(1)}, bf16[1,8,1024]{2,1,0:T(8,128)(2,1)S(1)}, u32[]{:S(2)}, u32[]{:S(2)}) collective-permute-start(bf16[1,8,1024]{2,1,0:T(8,128)(2,1)S(1)} %bitcast.8), channel_id=1, source_target_pairs={{0,12},{4,8},{8,0},{12,4},{1,13},{5,9},{9,1},{13,5},{2,14},{6,10},... | collective-permute-start | bytes 49160 | tf_op jit(solution)/shard_map/ppermute | solution.py:236
  8.5 3.7 %collective-permute-start = (bf16[1,8,1024]{2,1,0:T(8,128)(2,1)S(1)}, bf16[1,8,1024]{2,1,0:T(8,128)(2,1)S(1)}, u32[]{:S(2)}, u32[]{:S(2)}) collective-permute-start(bf16[1,8,1024]{2,1,0:T(8,128)(2,1)S(1)} %bitcast.9), channel_id=1, source_target_pairs={{0,4},{4,0},{8,12},{12,8},{1,5},{5,1},{9,13},{13,9},{2,6},{6,2},{1... | collective-permute-start | bytes 49160 | tf_op jit(solution)/shard_map/ppermute | solution.py:236
  13.0 1.4 %collective-permute-start.3 = (f32[208,128]{1,0:T(8,128)S(1)}, f32[208,128]{1,0:T(8,128)S(1)}, u32[]{:S(2)}, u32[]{:S(2)}) collective-permute-start(f32[208,128]{1,0:T(8,128)S(1)} %get-tuple-element.54), channel_id=1, source_target_pairs={{0,1},{1,0},{2,3},{3,2},{4,5},{5,4},{6,7},{7,6},{8,9},{9,8},{10,11... | collective-permute-start | bytes 319496 | tf_op jit(solution)/shard_map/ppermute | solution.py:220
  14.4 5.1 %collective-permute-start.6 = (bf16[208,128]{1,0:T(8,128)(2,1)S(1)}, bf16[208,128]{1,0:T(8,128)(2,1)S(1)}, u32[]{:S(2)}, u32[]{:S(2)}) collective-permute-start(bf16[208,128]{1,0:T(8,128)(2,1)S(1)} %add_convert_fusion.1), channel_id=1, source_target_pairs={{0,6},{1,7},{2,4},{3,5},{4,2},{5,3},{6,0},{7,1},{8,14},{9,15},{10,... | collective-permute-start | bytes 159752 | tf_op jit(solution)/shard_map/ppermute | solution.py:272
  16.8 4.1 %collective-permute-start.5 = (bf16[208,128]{1,0:T(8,128)(2,1)S(1)}, bf16[208,128]{1,0:T(8,128)(2,1)S(1)}, u32[]{:S(2)}, u32[]{:S(2)}) collective-permute-start(bf16[208,128]{1,0:T(8,128)(2,1)S(1)} %add_convert_fusion.1), channel_id=1, source_target_pairs={{0,5},{1,4},{2,7},{3,6},{4,1},{5,0},{6,3},{7,2},{8,12},{9,13},{10,... | collective-permute-start | bytes 159752 | tf_op jit(solution)/shard_map/ppermute | solution.py:272
  17.0 3.8 %collective-permute-start.4 = (bf16[208,128]{1,0:T(8,128)(2,1)S(1)}, bf16[208,128]{1,0:T(8,128)(2,1)S(1)}, u32[]{:S(2)}, u32[]{:S(2)}) collective-permute-start(bf16[208,128]{1,0:T(8,128)(2,1)S(1)} %add_convert_fusion.1), channel_id=1, source_target_pairs={{0,3},{1,2},{2,1},{3,0},{4,7},{5,6},{6,5},{7,4},{8,11},{9,10},{10,... | collective-permute-start | bytes 159752 | tf_op jit(solution)/shard_map/ppermute | solution.py:272
  20.9 4.6 %collective-permute-start.7 = (bf16[208,128]{1,0:T(8,128)(2,1)S(1)}, bf16[208,128]{1,0:T(8,128)(2,1)S(1)}, u32[]{:S(2)}, u32[]{:S(2)}) collective-permute-start(bf16[208,128]{1,0:T(8,128)(2,1)S(1)} %add_convert_fusion), channel_id=1, source_target_pairs={{0,9},{1,8},{2,11},{3,10},{4,14},{5,15},{6,13},{7,12},{8,1},{9,0},... | collective-permute-start | bytes 159752 | tf_op jit(solution)/shard_map/ppermute | solution.py:272
  25.6 1.4 %collective-permute-start.8 = (f32[208,128]{1,0:T(8,128)S(1)}, f32[208,128]{1,0:T(8,128)S(1)}, u32[]{:S(2)}, u32[]{:S(2)}) collective-permute-start(f32[208,128]{1,0:T(8,128)S(1)} %convert_add_fusion.total), channel_id=1, source_target_pairs={{0,1},{1,0},{2,3},{3,2},{4,5},{5,4},{6,7},{7,6},{8,9},{9,8},{10,11... | collective-permute-start | bytes 319496 | tf_op jit(solution)/shard_map/ppermute | solution.py:220

commit v5 on v4

--- a/solution.py
+++ b/solution.py
@@ -154,8 +154,8 @@
     @pl.when(step == steps - 1)
     def _():
         which = half_of_device()
-        keep[...] = rows[pl.ds(pl.multiple_of(which * half, 16), half), :]
-        away[...] = rows[pl.ds(pl.multiple_of((1 - which) * half, 16), half), :]
+        keep[...] = rows[pl.ds(pl.multiple_of(which * half, 8), half), :]
+        away[...] = rows[pl.ds(pl.multiple_of((1 - which) * half, 8), half), :]
 
 
 def score_kernel(parts, predicted, target, valid, *refs):
@@ -375,7 +375,7 @@
     )(latent_copy, observed_copy, valid_copy, pre_one, rise_one, hidden_one, pre_two, rise_two, gain_row)
 
     used = width + hidden + fields + members
-    half = -(-used // 32) * 16
+    half = -(-used // 16) * 8
     half_shape = jax.ShapeDtypeStruct((half, hidden), f32)
     keep, away = pl.pallas_call(
         functools.partial(

time: 27.9 us -> 27.7 us (level)
  waiting for transfers between devices: 9.93 us -> 9.65 us
where the time goes in v5:
time: 27.7 us; the launch traced here: 27.6 us
  starting transfers between devices  11.4 us (41%)
  waiting for transfers between devices  9.65 us (35%)
  Pallas kernels  5.13 us (19%)
  between operations  1.33 us (5%)
    ppermute x4, waiting for transfers between devices, cross(): return lax.ppermute(array, mesh_axes, pairs)  5.77 us
    ppermute x3, starting transfers between devices, gather_members(): lax.ppermute(block[None], 'member', list(enumerate(route)))  5.67 us
    ppermute x4, starting transfers between devices, cross(): return lax.ppermute(array, mesh_axes, pairs)  5.16 us
    ppermute x3, waiting for transfers between devices, gather_members(): lax.ppermute(block[None], 'member', list(enumerate(route)))  2.29 us
    pallas_call x1, Pallas kernels, on_device(): pl.pallas_call(functools.partial(forward_kernel, chunk), grid=(steps,), i...  2.05 us
    ppermute x2, waiting for transfers between devices, swap(): lax.ppermute(array, mesh_axes, [(place, place ^ offset) for place in rang...  1.6 us
    pallas_call x1, Pallas kernels, on_device(): pl.pallas_call(derivative_kernel, grid=(steps,), in_specs=[by_point((poin...  0.94 us
    pallas_call x1, Pallas kernels, on_device(): pl.pallas_call(functools.partial(backward_kernel, steps, norm_factor / me...  0.75 us
  transfers between devices with their start and end apart: 9, of which 8 were waited for; matrix products, arithmetic and copies ran while one was open for 0% of the time, Pallas kernels for 6%

profile of v5, /device:TPU:0, one launch (start us, length us, event | category | flops | bytes accessed | tf_op | source)
XLA Modules:
  0.0 27.6 jit_solution(6007654846651710080)
XLA Ops:
  1.3 2.1 %forward.1 = (bf16[1024,256]{1,0:T(8,128)(2,1)S(1)}, f32[8,4,256]{2,1,0:T(4,128)S(1)}, s32[4,256]{1,0:T(4,128)S(1)}, f32[1024,128]{1,0:T(8,128)S(1)}, f32[1024,1...) custom-call(s32[1,1]{1,0:T(1,128)S(6)} %copy.13.order, ...), custom_call_target="tpu_custom_call" | custom-call | tf_op jit(solution)/shard_map/forward/pallas_call | solution.py:340
  3.3 4.1 %collective-permute-start.2 = (bf16[1,8,1024]{2,1,0:T(8,128)(2,1)S(1)}, bf16[1,8,1024]{2,1,0:T(8,128)(2,1)S(1)}, u32[]{:S(2)}, u32[]{:S(2)}) collective-permute-start(bf16[1,8,1024]{2,1,0:T(8,128)(2,1)S(1)} %bitcast.7), channel_id=1, source_target_pairs={{0,8},{4,12},{8,4},{12,0},{1,9},{5,13},{9,5},{13,1},{2,10},{6,14},... | collective-permute-start | bytes 49160 | tf_op jit(solution)/shard_map/ppermute | solution.py:236
  7.4 1.1 %collective-permute-start.1 = (bf16[1,8,1024]{2,1,0:T(8,128)(2,1)S(1)}, bf16[1,8,1024]{2,1,0:T(8,128)(2,1)S(1)}, u32[]{:S(2)}, u32[]{:S(2)}) collective-permute-start(bf16[1,8,1024]{2,1,0:T(8,128)(2,1)S(1)} %bitcast.8), channel_id=1, source_target_pairs={{0,12},{4,8},{8,0},{12,4},{1,13},{5,9},{9,1},{13,5},{2,14},{6,10},... | collective-permute-start | bytes 49160 | tf_op jit(solution)/shard_map/ppermute | solution.py:236
  8.5 0.5 %collective-permute-start = (bf16[1,8,1024]{2,1,0:T(8,128)(2,1)S(1)}, bf16[1,8,1024]{2,1,0:T(8,128)(2,1)S(1)}, u32[]{:S(2)}, u32[]{:S(2)}) collective-permute-start(bf16[1,8,1024]{2,1,0:T(8,128)(2,1)S(1)} %bitcast.9), channel_id=1, source_target_pairs={{0,4},{4,0},{8,12},{12,8},{1,5},{5,1},{9,13},{13,9},{2,6},{6,2},{1... | collective-permute-start | bytes 49160 | tf_op jit(solution)/shard_map/ppermute | solution.py:236
  9.0 0.9 %derivatives.1 = (f32[1024,128]{1,0:T(8,128)S(1)}, f32[1024,128]{1,0:T(8,128)S(1)}, f32[1024,128]{1,0:T(8,128)S(1)}, bf16[256,1024]{1,0:T(8,128)(2,1)S(1)}, bf16...) custom-call(bf16[1024,256]{1,0:T(8,128)(2,1)S(1)} %get-tuple-element.33.latent, ...), custom_call_target="tpu_custom_call" | custom-call | tf_op jit(solution)/shard_map/derivatives/pallas_call | solution.py:366
  10.0 0.2 collective-permute-done.2.refs_2_.refs_5_
  10.2 1.9 %collective-permute-done.1.refs_1_.refs_4_ = bf16[1,8,1024]{2,1,0:T(8,128)(2,1)S(1)} collective-permute-done((bf16[1,8,1024]{2,1,0:T(8,128)(2,1)S(1)}, bf16[1,8,1024]{2,1,0:T(8,128)(2,1)S(1)}, u32[]{:S(2)}, u32[]{:S(2)}) %collective-permute-start.1) | collective-permute-done | bytes 16416 | tf_op jit(solution)/shard_map/ppermute | solution.py:236
  12.1 0.2 collective-permute-done.refs_0_.refs_3_
  12.2 0.7 %backward.1 = (f32[200,128]{1,0:T(8,128)S(1)}, f32[200,128]{1,0:T(8,128)S(1)}) custom-call(s32[1,1]{1,0:T(1,128)S(6)} %copy.13.order, f32[8,1024]{1,0:T(8,128)S(1)} %get-tuple-element.32.predicted.refs_0_, f32[8,1024]{1,0:T(8,128)S(1)} %get-tuple-element.42.target.refs_1_, f32[1,1024]{1,0:T(1,128)S(1)} %get-tuple-element.43.valid.refs_2_, ...), custom_call_target="tpu_custom_call" | custom-call | tf_op jit(solution)/shard_map/backward/pallas_call | solution.py:380
  13.0 0.1 collective-permute-start.3
  13.1 1.3 %collective-permute-done.3 = f32[200,128]{1,0:T(8,128)S(1)} collective-permute-done((f32[200,128]{1,0:T(8,128)S(1)}, f32[200,128]{1,0:T(8,128)S(1)}, u32[]{:S(2)}, u32[]{:S(2)}) %collective-permute-start.3) | collective-permute-done | bytes 102432 | tf_op jit(solution)/shard_map/ppermute | solution.py:220
  14.4 2.4 %collective-permute-start.6 = (bf16[200,128]{1,0:T(8,128)(2,1)S(1)}, bf16[200,128]{1,0:T(8,128)(2,1)S(1)}, u32[]{:S(2)}, u32[]{:S(2)}) collective-permute-start(bf16[200,128]{1,0:T(8,128)(2,1)S(1)} %add_convert_fusion.1), channel_id=1, source_target_pairs={{0,6},{1,7},{2,4},{3,5},{4,2},{5,3},{6,0},{7,1},{8,14},{9,15},{10,... | collective-permute-start | bytes 153608 | tf_op jit(solution)/shard_map/ppermute | solution.py:272
  16.8 0.3 collective-permute-start.5
  17.0 0.6 %collective-permute-start.4 = (bf16[200,128]{1,0:T(8,128)(2,1)S(1)}, bf16[200,128]{1,0:T(8,128)(2,1)S(1)}, u32[]{:S(2)}, u32[]{:S(2)}) collective-permute-start(bf16[200,128]{1,0:T(8,128)(2,1)S(1)} %add_convert_fusion.1), channel_id=1, source_target_pairs={{0,3},{1,2},{2,1},{3,0},{4,7},{5,6},{6,5},{7,4},{8,11},{9,10},{10,... | collective-permute-start | bytes 153608 | tf_op jit(solution)/shard_map/ppermute | solution.py:272
  17.7 1.8 %collective-permute-done.6 = bf16[200,128]{1,0:T(8,128)(2,1)S(1)} collective-permute-done((bf16[200,128]{1,0:T(8,128)(2,1)S(1)}, bf16[200,128]{1,0:T(8,128)(2,1)S(1)}, u32[]{:S(2)}, u32[]{:S(2)}) %collective-permute-start.6) | collective-permute-done | bytes 51232 | tf_op jit(solution)/shard_map/ppermute | solution.py:272
  19.5 1.3 %collective-permute-done.5 = bf16[200,128]{1,0:T(8,128)(2,1)S(1)} collective-permute-done((bf16[200,128]{1,0:T(8,128)(2,1)S(1)}, bf16[200,128]{1,0:T(8,128)(2,1)S(1)}, u32[]{:S(2)}, u32[]{:S(2)}) %collective-permute-start.5) | collective-permute-done | bytes 51232 | tf_op jit(solution)/shard_map/ppermute | solution.py:272
  20.8 0.0 collective-permute-done.4
  20.9 1.9 %collective-permute-start.7 = (bf16[200,128]{1,0:T(8,128)(2,1)S(1)}, bf16[200,128]{1,0:T(8,128)(2,1)S(1)}, u32[]{:S(2)}, u32[]{:S(2)}) collective-permute-start(bf16[200,128]{1,0:T(8,128)(2,1)S(1)} %add_convert_fusion), channel_id=1, source_target_pairs={{0,9},{1,8},{2,11},{3,10},{4,14},{5,15},{6,13},{7,12},{8,1},{9,0},... | collective-permute-start | bytes 153608 | tf_op jit(solution)/shard_map/ppermute | solution.py:272
  22.7 2.6 %collective-permute-done.7 = bf16[200,128]{1,0:T(8,128)(2,1)S(1)} collective-permute-done((bf16[200,128]{1,0:T(8,128)(2,1)S(1)}, bf16[200,128]{1,0:T(8,128)(2,1)S(1)}, u32[]{:S(2)}, u32[]{:S(2)}) %collective-permute-start.7) | collective-permute-done | bytes 51232 | tf_op jit(solution)/shard_map/ppermute | solution.py:272
  25.4 0.5 %collective-permute-start.8 = (f32[200,128]{1,0:T(8,128)S(1)}, f32[200,128]{1,0:T(8,128)S(1)}, u32[]{:S(2)}, u32[]{:S(2)}) collective-permute-start(f32[200,128]{1,0:T(8,128)S(1)} %convert_add_fusion.total), channel_id=1, source_target_pairs={{0,1},{1,0},{2,3},{3,2},{4,5},{5,4},{6,7},{7,6},{8,9},{9,8},{10,11... | collective-permute-start | bytes 307208 | tf_op jit(solution)/shard_map/ppermute | solution.py:220
  25.9 0.6 %score.1 = f32[8,1,256]{2,1,0:T(1,128)} custom-call(f32[8,1024]{1,0:T(8,128)S(1)} %get-tuple-element.32.predicted.refs_0_, f32[8,1024]{1,0:T(8,128)S(1)} %get-tuple-element.42.target.refs_1_, f32[1,1024]{1,0:T(1,128)S(1)} %get-tuple-element.43.valid.refs_2_, bf16[1,8,1024]{2,1,0:T(8,128)(2,1)S(1)} %collective-permute-done.refs_0_.refs_3_, ...), custom_call_target="tpu_custom_call" | custom-call | tf_op jit(solution)/shard_map/score/pallas_call | solution.py:406
  26.5 0.3 %collective-permute-done.8.other = f32[200,128]{1,0:T(8,128)S(1)} collective-permute-done((f32[200,128]{1,0:T(8,128)S(1)}, f32[200,128]{1,0:T(8,128)S(1)}, u32[]{:S(2)}, u32[]{:S(2)}) %collective-permute-start.8) | collective-permute-done | bytes 102432 | tf_op jit(solution)/shard_map/ppermute | solution.py:220
  26.8 0.7 %gradients.1 = (f32[256,128]{1,0:T(8,128)}, f32[128,128]{1,0:T(8,128)}, f32[8,128]{1,0:T(8,128)}, f32[4,128]{1,0:T(4,128)}) custom-call(f32[200,128]{1,0:T(8,128)S(1)} %convert_add_fusion.total, f32[200,128]{1,0:T(8,128)S(1)} %collective-permute-done.8.other), custom_call_target="tpu_custom_call" | custom-call | tf_op jit(solution)/shard_map/gradients/pallas_call | solution.py:418
  (3 shorter events, 0.1 us)
Async XLA Ops:
  3.3 6.8 %collective-permute-start.2 = (bf16[1,8,1024]{2,1,0:T(8,128)(2,1)S(1)}, bf16[1,8,1024]{2,1,0:T(8,128)(2,1)S(1)}, u32[]{:S(2)}, u32[]{:S(2)}) collective-permute-start(bf16[1,8,1024]{2,1,0:T(8,128)(2,1)S(1)} %bitcast.7), channel_id=1, source_target_pairs={{0,8},{4,12},{8,4},{12,0},{1,9},{5,13},{9,5},{13,1},{2,10},{6,14},... | collective-permute-start | bytes 49160 | tf_op jit(solution)/shard_map/ppermute | solution.py:236
  7.4 4.6 %collective-permute-start.1 = (bf16[1,8,1024]{2,1,0:T(8,128)(2,1)S(1)}, bf16[1,8,1024]{2,1,0:T(8,128)(2,1)S(1)}, u32[]{:S(2)}, u32[]{:S(2)}) collective-permute-start(bf16[1,8,1024]{2,1,0:T(8,128)(2,1)S(1)} %bitcast.8), channel_id=1, source_target_pairs={{0,12},{4,8},{8,0},{12,4},{1,13},{5,9},{9,1},{13,5},{2,14},{6,10},... | collective-permute-start | bytes 49160 | tf_op jit(solution)/shard_map/ppermute | solution.py:236
  8.5 3.7 %collective-permute-start = (bf16[1,8,1024]{2,1,0:T(8,128)(2,1)S(1)}, bf16[1,8,1024]{2,1,0:T(8,128)(2,1)S(1)}, u32[]{:S(2)}, u32[]{:S(2)}) collective-permute-start(bf16[1,8,1024]{2,1,0:T(8,128)(2,1)S(1)} %bitcast.9), channel_id=1, source_target_pairs={{0,4},{4,0},{8,12},{12,8},{1,5},{5,1},{9,13},{13,9},{2,6},{6,2},{1... | collective-permute-start | bytes 49160 | tf_op jit(solution)/shard_map/ppermute | solution.py:236
  13.0 1.4 %collective-permute-start.3 = (f32[200,128]{1,0:T(8,128)S(1)}, f32[200,128]{1,0:T(8,128)S(1)}, u32[]{:S(2)}, u32[]{:S(2)}) collective-permute-start(f32[200,128]{1,0:T(8,128)S(1)} %get-tuple-element.54), channel_id=1, source_target_pairs={{0,1},{1,0},{2,3},{3,2},{4,5},{5,4},{6,7},{7,6},{8,9},{9,8},{10,11... | collective-permute-start | bytes 307208 | tf_op jit(solution)/shard_map/ppermute | solution.py:220
  14.4 5.1 %collective-permute-start.6 = (bf16[200,128]{1,0:T(8,128)(2,1)S(1)}, bf16[200,128]{1,0:T(8,128)(2,1)S(1)}, u32[]{:S(2)}, u32[]{:S(2)}) collective-permute-start(bf16[200,128]{1,0:T(8,128)(2,1)S(1)} %add_convert_fusion.1), channel_id=1, source_target_pairs={{0,6},{1,7},{2,4},{3,5},{4,2},{5,3},{6,0},{7,1},{8,14},{9,15},{10,... | collective-permute-start | bytes 153608 | tf_op jit(solution)/shard_map/ppermute | solution.py:272
  16.8 4.0 %collective-permute-start.5 = (bf16[200,128]{1,0:T(8,128)(2,1)S(1)}, bf16[200,128]{1,0:T(8,128)(2,1)S(1)}, u32[]{:S(2)}, u32[]{:S(2)}) collective-permute-start(bf16[200,128]{1,0:T(8,128)(2,1)S(1)} %add_convert_fusion.1), channel_id=1, source_target_pairs={{0,5},{1,4},{2,7},{3,6},{4,1},{5,0},{6,3},{7,2},{8,12},{9,13},{10,... | collective-permute-start | bytes 153608 | tf_op jit(solution)/shard_map/ppermute | solution.py:272
  17.0 3.8 %collective-permute-start.4 = (bf16[200,128]{1,0:T(8,128)(2,1)S(1)}, bf16[200,128]{1,0:T(8,128)(2,1)S(1)}, u32[]{:S(2)}, u32[]{:S(2)}) collective-permute-start(bf16[200,128]{1,0:T(8,128)(2,1)S(1)} %add_convert_fusion.1), channel_id=1, source_target_pairs={{0,3},{1,2},{2,1},{3,0},{4,7},{5,6},{6,5},{7,4},{8,11},{9,10},{10,... | collective-permute-start | bytes 153608 | tf_op jit(solution)/shard_map/ppermute | solution.py:272
  20.9 4.5 %collective-permute-start.7 = (bf16[200,128]{1,0:T(8,128)(2,1)S(1)}, bf16[200,128]{1,0:T(8,128)(2,1)S(1)}, u32[]{:S(2)}, u32[]{:S(2)}) collective-permute-start(bf16[200,128]{1,0:T(8,128)(2,1)S(1)} %add_convert_fusion), channel_id=1, source_target_pairs={{0,9},{1,8},{2,11},{3,10},{4,14},{5,15},{6,13},{7,12},{8,1},{9,0},... | collective-permute-start | bytes 153608 | tf_op jit(solution)/shard_map/ppermute | solution.py:272
  25.4 1.4 %collective-permute-start.8 = (f32[200,128]{1,0:T(8,128)S(1)}, f32[200,128]{1,0:T(8,128)S(1)}, u32[]{:S(2)}, u32[]{:S(2)}) collective-permute-start(f32[200,128]{1,0:T(8,128)S(1)} %convert_add_fusion.total), channel_id=1, source_target_pairs={{0,1},{1,0},{2,3},{3,2},{4,5},{5,4},{6,7},{7,6},{8,9},{9,8},{10,11... | collective-permute-start | bytes 307208 | tf_op jit(solution)/shard_map/ppermute | solution.py:220

commit v6 on v5

--- a/solution.py
+++ b/solution.py
@@ -158,6 +158,60 @@
         away[...] = rows[pl.ds(pl.multiple_of((1 - which) * half, 8), half), :]
 
 
+def fill_half(half_rows, side, order, latent_t, hidden_t, hidden_two, grad_pre_one, grad_pre_two, flat, gain_sum):
+    half, width, hidden, fields = half_rows.shape[0], latent_t.shape[0], hidden_t.shape[0], flat.shape[0]
+    if side == 0:
+        upper = -(-half // 16) * 16
+        part = jnp.dot(latent_t[0:upper, :], grad_pre_one[...], preferred_element_type=f32)
+        half_rows[...] = part[:half]
+        return
+    lower = half // 16 * 16
+    part = jnp.dot(latent_t[lower:width, :], grad_pre_one[...], preferred_element_type=f32)
+    first = width - half
+    half_rows[0:first, :] = part[half - lower :]
+    half_rows[first : first + hidden, :] = jnp.dot(hidden_t[...], grad_pre_two[...], preferred_element_type=f32)
+    first += hidden
+    half_rows[first : first + fields, :] = jnp.dot(flat[...], hidden_two[...], preferred_element_type=f32)
+    first += fields
+    spots = lax.broadcasted_iota(jnp.int32, (half - first, 1), 0)
+    half_rows[first:half, :] = jnp.where(spots == order[0, 0], gain_sum[...], 0.0)
+
+
+def away_kernel(scale_own, scale_pair, parts, order, *refs):
+    (predicted, target, valid), refs = refs[:3], refs[3:]
+    ensemble, refs = refs[:parts], refs[parts:]
+    latent_t, hidden_t, hidden_two, act_one, slope_one, slope_two, weight_mid, weight_out = refs[:8]
+    away, grad_pre_one, grad_pre_two, flat, gain_sum = refs[8:]
+    mine = predicted[...]
+    slopes = sum(soft_slope(mine - part[0].astype(f32)) for part in ensemble)
+    grad = valid[...] * (soft_slope(mine - target[...]) * scale_own - slopes * scale_pair)
+    flat[...] = grad.astype(bf16)
+    grad_hid_two = lax.dot_general(
+        flat[...], weight_out[...], (((0,), (0,)), ((), ())), preferred_element_type=f32
+    )
+    grad_pre_two[...] = (grad_hid_two * slope_two[...]).astype(bf16)
+    grad_hid_one = lax.dot_general(
+        grad_pre_two[...], weight_mid[...], (((1,), (1,)), ((), ())), preferred_element_type=f32
+    )
+    grad_pre_one[...] = (grad_hid_one * slope_one[...]).astype(bf16)
+    gain_sum[...] = jnp.sum(grad_hid_one * act_one[...], axis=0, keepdims=True)
+    which = half_of_device()
+    for side in range(2):
+
+        @pl.when(which != side)
+        def _():
+            fill_half(away, side, order, latent_t, hidden_t, hidden_two, grad_pre_one, grad_pre_two, flat, gain_sum)
+
+
+def keep_kernel(order, latent_t, hidden_t, hidden_two, grad_pre_one, grad_pre_two, flat, gain_sum, keep):
+    which = half_of_device()
+    for side in range(2):
+
+        @pl.when(which == side)
+        def _():
+            fill_half(keep, side, order, latent_t, hidden_t, hidden_two, grad_pre_one, grad_pre_two, flat, gain_sum)
+
+
 def score_kernel(parts, predicted, target, valid, *refs):
     ensemble, score = refs[:parts], refs[parts]
     fields, rows, cols = score.shape
@@ -377,29 +431,59 @@
     used = width + hidden + fields + members
     half = -(-used // 16) * 8
     half_shape = jax.ShapeDtypeStruct((half, hidden), f32)
-    keep, away = pl.pallas_call(
-        functools.partial(
-            backward_kernel,
-            steps,
-            norm_factor / members,
-            norm_factor / (members * (members - 1.0)),
-            len(parts),
-        ),
-        grid=(steps,),
-        in_specs=[smem, wide_spec, wide_spec, by_lane((1, points))]
-        + [by_lane(part.shape) for part in parts]
-        + [by_lane((width, points)), by_lane((hidden, points))]
-        + [tall_spec] * 4
-        + [whole_spec(weight_mid), whole_spec(weight_out_t)],
-        out_specs=[whole_spec(half_shape)] * 2,
-        out_shape=[half_shape] * 2,
-        scratch_shapes=[pltpu.VMEM((2 * half, hidden), f32)],
-        compiler_params=kernel_params,
-        name="backward",
-    )(
-        member_order, predicted, target, is_valid, *parts, latent_t, hidden_t,
-        hidden_two, act_one, slope_one, slope_two, mid_copy, out_copy,
-    )
+    scales = (norm_factor / members, norm_factor / (members * (members - 1.0)), len(parts))
+    if steps == 1 and all(part.shape[0] == 1 for part in parts) and half <= width:
+        middle = [tall(bf16), tall(bf16), wide(fields, bf16), gain_shape]
+        away, *middle_arrays = pl.pallas_call(
+            functools.partial(away_kernel, *scales),
+            grid=(steps,),
+            in_specs=[smem, wide_spec, wide_spec, by_lane((1, points))]
+            + [by_lane(part.shape) for part in parts]
+            + [by_lane((width, points)), by_lane((hidden, points))]
+            + [tall_spec] * 4
+            + [whole_spec(weight_mid), whole_spec(weight_out_t)],
+            out_specs=[whole_spec(half_shape)] + [whole_spec(shape) for shape in middle],
+            out_shape=[half_shape] + middle,
+            compiler_params=kernel_params,
+            name="away",
+        )(
+            member_order, predicted, target, is_valid, *parts, latent_t, hidden_t,
+            hidden_two, act_one, slope_one, slope_two, mid_copy, out_copy,
+        )
+        rest = (latent_t, hidden_t, hidden_two, *middle_arrays)
+        keep = pl.pallas_call(
+            keep_kernel,
+            grid=(1,),
+            in_specs=[smem] + [whole_spec(array) for array in rest],
+            out_specs=whole_spec(half_shape),
+            out_shape=half_shape,
+            compiler_params=kernel_params,
+            name="keep",
+        )(member_order, *rest)
+    else:
+        keep, away = pl.pallas_call(
+            functools.partial(
+                backward_kernel,
+                steps,
+                norm_factor / members,
+                norm_factor / (members * (members - 1.0)),
+                len(parts),
+            ),
+            grid=(steps,),
+            in_specs=[smem, wide_spec, wide_spec, by_lane((1, points))]
+            + [by_lane(part.shape) for part in parts]
+            + [by_lane((width, points)), by_lane((hidden, points))]
+            + [tall_spec] * 4
+            + [whole_spec(weight_mid), whole_spec(weight_out_t)],
+            out_specs=[whole_spec(half_shape)] * 2,
+            out_shape=[half_shape] * 2,
+            scratch_shapes=[pltpu.VMEM((2 * half, hidden), f32)],
+            compiler_params=kernel_params,
+            name="backward",
+        )(
+            member_order, predicted, target, is_valid, *parts, latent_t, hidden_t,
+            hidden_two, act_one, slope_one, slope_two, mid_copy, out_copy,
+        )
 
     score_shape = jax.ShapeDtypeStruct((fields, row_count // members, tile_cols), f32)
     score_inputs = (predicted, target, is_valid, *parts)

time: 27.7 us -> 27.8 us (level)
  Pallas kernels: 5.13 us -> 5.45 us
  waiting for transfers between devices: 9.65 us -> 9.34 us
    pallas_call x1 -> x2, Pallas kernels: 0.75 us -> 1.07 us  [the longest x1 0.77 us: on_device(): pl.pallas_call(functools.partial(away_kernel, *scales), grid=(steps,), in...]
    ppermute x2, waiting for transfers between devices: 1.6 us -> 1.3 us  [swap(): lax.ppermute(array, mesh_axes, [(place, place ^ offset) for place in rang...]
  transfers between devices with their start and end apart: 9 -> 9, of which waited for: 8 -> 8; matrix products, arithmetic and copies ran while one was open for 0% -> 0% of each run, Pallas kernels for 6% -> 7%
where the time goes in v6:
time: 27.8 us; the launch traced here: 27.6 us
  starting transfers between devices  11.4 us (41%)
  waiting for transfers between devices  9.34 us (34%)
  Pallas kernels  5.45 us (20%)
  between operations  1.33 us (5%)
    ppermute x4, waiting for transfers between devices, cross(): return lax.ppermute(array, mesh_axes, pairs)  5.75 us
    ppermute x3, starting transfers between devices, gather_members(): lax.ppermute(block[None], 'member', list(enumerate(route)))  5.67 us
    ppermute x4, starting transfers between devices, cross(): return lax.ppermute(array, mesh_axes, pairs)  5.18 us
    ppermute x3, waiting for transfers between devices, gather_members(): lax.ppermute(block[None], 'member', list(enumerate(route)))  2.29 us
    pallas_call x1, Pallas kernels, on_device(): pl.pallas_call(functools.partial(forward_kernel, chunk), grid=(steps,), i...  2.05 us
    ppermute x2, waiting for transfers between devices, swap(): lax.ppermute(array, mesh_axes, [(place, place ^ offset) for place in rang...  1.3 us
    pallas_call x1, Pallas kernels, on_device(): pl.pallas_call(derivative_kernel, grid=(steps,), in_specs=[by_point((poin...  0.94 us
    pallas_call x1, Pallas kernels, on_device(): pl.pallas_call(functools.partial(away_kernel, *scales), grid=(steps,), in...  0.77 us
  transfers between devices with their start and end apart: 9, of which 8 were waited for; matrix products, arithmetic and copies ran while one was open for 0% of the time, Pallas kernels for 7%

profile of v6, /device:TPU:0, one launch (start us, length us, event | category | flops | bytes accessed | tf_op | source)
XLA Modules:
  0.0 27.6 jit_solution(9825481765120602925)
XLA Ops:
  1.3 2.1 %forward.1 = (bf16[1024,256]{1,0:T(8,128)(2,1)S(1)}, f32[8,4,256]{2,1,0:T(4,128)S(1)}, s32[4,256]{1,0:T(4,128)S(1)}, f32[1024,128]{1,0:T(8,128)S(1)}, f32[1024,1...) custom-call(s32[1,1]{1,0:T(1,128)S(6)} %copy.13.order, ...), custom_call_target="tpu_custom_call" | custom-call | tf_op jit(solution)/shard_map/forward/pallas_call | solution.py:394
  3.3 4.1 %collective-permute-start.2 = (bf16[1,8,1024]{2,1,0:T(8,128)(2,1)S(1)}, bf16[1,8,1024]{2,1,0:T(8,128)(2,1)S(1)}, u32[]{:S(2)}, u32[]{:S(2)}) collective-permute-start(bf16[1,8,1024]{2,1,0:T(8,128)(2,1)S(1)} %bitcast.7), channel_id=1, source_target_pairs={{0,8},{4,12},{8,4},{12,0},{1,9},{5,13},{9,5},{13,1},{2,10},{6,14},... | collective-permute-start | bytes 49160 | tf_op jit(solution)/shard_map/ppermute | solution.py:290
  7.4 1.1 %collective-permute-start.1 = (bf16[1,8,1024]{2,1,0:T(8,128)(2,1)S(1)}, bf16[1,8,1024]{2,1,0:T(8,128)(2,1)S(1)}, u32[]{:S(2)}, u32[]{:S(2)}) collective-permute-start(bf16[1,8,1024]{2,1,0:T(8,128)(2,1)S(1)} %bitcast.8), channel_id=1, source_target_pairs={{0,12},{4,8},{8,0},{12,4},{1,13},{5,9},{9,1},{13,5},{2,14},{6,10},... | collective-permute-start | bytes 49160 | tf_op jit(solution)/shard_map/ppermute | solution.py:290
  8.5 0.5 %collective-permute-start = (bf16[1,8,1024]{2,1,0:T(8,128)(2,1)S(1)}, bf16[1,8,1024]{2,1,0:T(8,128)(2,1)S(1)}, u32[]{:S(2)}, u32[]{:S(2)}) collective-permute-start(bf16[1,8,1024]{2,1,0:T(8,128)(2,1)S(1)} %bitcast.9), channel_id=1, source_target_pairs={{0,4},{4,0},{8,12},{12,8},{1,5},{5,1},{9,13},{13,9},{2,6},{6,2},{1... | collective-permute-start | bytes 49160 | tf_op jit(solution)/shard_map/ppermute | solution.py:290
  9.0 0.9 %derivatives.1 = (f32[1024,128]{1,0:T(8,128)S(1)}, f32[1024,128]{1,0:T(8,128)S(1)}, f32[1024,128]{1,0:T(8,128)S(1)}, bf16[256,1024]{1,0:T(8,128)(2,1)S(1)}, bf16...) custom-call(bf16[1024,256]{1,0:T(8,128)(2,1)S(1)} %get-tuple-element.36.latent, ...), custom_call_target="tpu_custom_call" | custom-call | tf_op jit(solution)/shard_map/derivatives/pallas_call | solution.py:420
  10.0 0.2 collective-permute-done.2.refs_2_.refs_5_
  10.2 1.9 %collective-permute-done.1.refs_1_.refs_4_ = bf16[1,8,1024]{2,1,0:T(8,128)(2,1)S(1)} collective-permute-done((bf16[1,8,1024]{2,1,0:T(8,128)(2,1)S(1)}, bf16[1,8,1024]{2,1,0:T(8,128)(2,1)S(1)}, u32[]{:S(2)}, u32[]{:S(2)}) %collective-permute-start.1) | collective-permute-done | bytes 16416 | tf_op jit(solution)/shard_map/ppermute | solution.py:290
  12.1 0.2 collective-permute-done.refs_0_.refs_3_
  12.2 0.8 %away.1 = (f32[200,128]{1,0:T(8,128)S(1)}, bf16[1024,128]{1,0:T(8,128)(2,1)S(1)}, bf16[1024,128]{1,0:T(8,128)(2,1)S(1)}, bf16[8,1024]{1,0:T(8,128)(2,1)S(1)}, f32[1,128]{1,0:T(1,128)S(1)}) custom-call(s32[1,1]{1,0:T(1,128)S(6)} %copy.13.order, f32[8,1024]{1,0:T(8,128)S(1)} %get-tuple-element.35.predicted.refs_0_, ...), custom_call_target="tpu_custom_call" | custom-call | tf_op jit(solution)/shard_map/away/pallas_call | solution.py:437
  13.0 0.1 collective-permute-start.3
  13.1 0.3 %keep.1 = f32[200,128]{1,0:T(8,128)S(1)} custom-call(s32[1,1]{1,0:T(1,128)S(6)} %copy.13.order, bf16[256,1024]{1,0:T(8,128)(2,1)S(1)} %get-tuple-element.48.refs_6_.latent_t, bf16[128,1024]{1,0:T(8,128)(2,1)S(1)} %get-tuple-element.49.refs_7_.hidden_t, bf16[1024,128]{1,0:T(8,128)(2,1)S(1)} %get-tuple-element.50.refs_8_.hidden_two, ...), custom_call_target="tpu_custom_call" | custom-call | tf_op jit(solution)/shard_map/keep/pallas_call | solution.py:454
  13.4 1.0 %collective-permute-done.3 = f32[200,128]{1,0:T(8,128)S(1)} collective-permute-done((f32[200,128]{1,0:T(8,128)S(1)}, f32[200,128]{1,0:T(8,128)S(1)}, u32[]{:S(2)}, u32[]{:S(2)}) %collective-permute-start.3) | collective-permute-done | bytes 102432 | tf_op jit(solution)/shard_map/ppermute | solution.py:274
  14.4 2.4 %collective-permute-start.6 = (bf16[200,128]{1,0:T(8,128)(2,1)S(1)}, bf16[200,128]{1,0:T(8,128)(2,1)S(1)}, u32[]{:S(2)}, u32[]{:S(2)}) collective-permute-start(bf16[200,128]{1,0:T(8,128)(2,1)S(1)} %add_convert_fusion.1), channel_id=1, source_target_pairs={{0,6},{1,7},{2,4},{3,5},{4,2},{5,3},{6,0},{7,1},{8,14},{9,15},{10,... | collective-permute-start | bytes 153608 | tf_op jit(solution)/shard_map/ppermute | solution.py:326
  16.8 0.3 %collective-permute-start.5 = (bf16[200,128]{1,0:T(8,128)(2,1)S(1)}, bf16[200,128]{1,0:T(8,128)(2,1)S(1)}, u32[]{:S(2)}, u32[]{:S(2)}) collective-permute-start(bf16[200,128]{1,0:T(8,128)(2,1)S(1)} %add_convert_fusion.1), channel_id=1, source_target_pairs={{0,5},{1,4},{2,7},{3,6},{4,1},{5,0},{6,3},{7,2},{8,12},{9,13},{10,... | collective-permute-start | bytes 153608 | tf_op jit(solution)/shard_map/ppermute | solution.py:326
  17.1 0.6 %collective-permute-start.4 = (bf16[200,128]{1,0:T(8,128)(2,1)S(1)}, bf16[200,128]{1,0:T(8,128)(2,1)S(1)}, u32[]{:S(2)}, u32[]{:S(2)}) collective-permute-start(bf16[200,128]{1,0:T(8,128)(2,1)S(1)} %add_convert_fusion.1), channel_id=1, source_target_pairs={{0,3},{1,2},{2,1},{3,0},{4,7},{5,6},{6,5},{7,4},{8,11},{9,10},{10,... | collective-permute-start | bytes 153608 | tf_op jit(solution)/shard_map/ppermute | solution.py:326
  17.7 1.8 %collective-permute-done.6 = bf16[200,128]{1,0:T(8,128)(2,1)S(1)} collective-permute-done((bf16[200,128]{1,0:T(8,128)(2,1)S(1)}, bf16[200,128]{1,0:T(8,128)(2,1)S(1)}, u32[]{:S(2)}, u32[]{:S(2)}) %collective-permute-start.6) | collective-permute-done | bytes 51232 | tf_op jit(solution)/shard_map/ppermute | solution.py:326
  19.5 1.4 %collective-permute-done.5 = bf16[200,128]{1,0:T(8,128)(2,1)S(1)} collective-permute-done((bf16[200,128]{1,0:T(8,128)(2,1)S(1)}, bf16[200,128]{1,0:T(8,128)(2,1)S(1)}, u32[]{:S(2)}, u32[]{:S(2)}) %collective-permute-start.5) | collective-permute-done | bytes 51232 | tf_op jit(solution)/shard_map/ppermute | solution.py:326
  20.8 0.0 collective-permute-done.4
  20.9 1.9 %collective-permute-start.7 = (bf16[200,128]{1,0:T(8,128)(2,1)S(1)}, bf16[200,128]{1,0:T(8,128)(2,1)S(1)}, u32[]{:S(2)}, u32[]{:S(2)}) collective-permute-start(bf16[200,128]{1,0:T(8,128)(2,1)S(1)} %add_convert_fusion), channel_id=1, source_target_pairs={{0,9},{1,8},{2,11},{3,10},{4,14},{5,15},{6,13},{7,12},{8,1},{9,0},... | collective-permute-start | bytes 153608 | tf_op jit(solution)/shard_map/ppermute | solution.py:326
  22.8 2.6 %collective-permute-done.7 = bf16[200,128]{1,0:T(8,128)(2,1)S(1)} collective-permute-done((bf16[200,128]{1,0:T(8,128)(2,1)S(1)}, bf16[200,128]{1,0:T(8,128)(2,1)S(1)}, u32[]{:S(2)}, u32[]{:S(2)}) %collective-permute-start.7) | collective-permute-done | bytes 51232 | tf_op jit(solution)/shard_map/ppermute | solution.py:326
  25.4 0.5 %collective-permute-start.8 = (f32[200,128]{1,0:T(8,128)S(1)}, f32[200,128]{1,0:T(8,128)S(1)}, u32[]{:S(2)}, u32[]{:S(2)}) collective-permute-start(f32[200,128]{1,0:T(8,128)S(1)} %convert_add_fusion.total), channel_id=1, source_target_pairs={{0,1},{1,0},{2,3},{3,2},{4,5},{5,4},{6,7},{7,6},{8,9},{9,8},{10,11... | collective-permute-start | bytes 307208 | tf_op jit(solution)/shard_map/ppermute | solution.py:274
  25.9 0.6 %score.1 = f32[8,1,256]{2,1,0:T(1,128)} custom-call(f32[8,1024]{1,0:T(8,128)S(1)} %get-tuple-element.35.predicted.refs_0_, f32[8,1024]{1,0:T(8,128)S(1)} %get-tuple-element.45.target.refs_1_, f32[1,1024]{1,0:T(1,128)S(1)} %get-tuple-element.46.valid.refs_2_, bf16[1,8,1024]{2,1,0:T(8,128)(2,1)S(1)} %collective-permute-done.refs_0_.refs_3_, ...), custom_call_target="tpu_custom_call" | custom-call | tf_op jit(solution)/shard_map/score/pallas_call | solution.py:490
  26.6 0.3 %collective-permute-done.8.other = f32[200,128]{1,0:T(8,128)S(1)} collective-permute-done((f32[200,128]{1,0:T(8,128)S(1)}, f32[200,128]{1,0:T(8,128)S(1)}, u32[]{:S(2)}, u32[]{:S(2)}) %collective-permute-start.8) | collective-permute-done | bytes 102432 | tf_op jit(solution)/shard_map/ppermute | solution.py:274
  26.9 0.7 %gradients.1 = (f32[256,128]{1,0:T(8,128)}, f32[128,128]{1,0:T(8,128)}, f32[8,128]{1,0:T(8,128)}, f32[4,128]{1,0:T(4,128)}) custom-call(f32[200,128]{1,0:T(8,128)S(1)} %convert_add_fusion.total, f32[200,128]{1,0:T(8,128)S(1)} %collective-permute-done.8.other), custom_call_target="tpu_custom_call" | custom-call | tf_op jit(solution)/shard_map/gradients/pallas_call | solution.py:502
  (3 shorter events, 0.1 us)
Async XLA Ops:
  3.3 6.8 %collective-permute-start.2 = (bf16[1,8,1024]{2,1,0:T(8,128)(2,1)S(1)}, bf16[1,8,1024]{2,1,0:T(8,128)(2,1)S(1)}, u32[]{:S(2)}, u32[]{:S(2)}) collective-permute-start(bf16[1,8,1024]{2,1,0:T(8,128)(2,1)S(1)} %bitcast.7), channel_id=1, source_target_pairs={{0,8},{4,12},{8,4},{12,0},{1,9},{5,13},{9,5},{13,1},{2,10},{6,14},... | collective-permute-start | bytes 49160 | tf_op jit(solution)/shard_map/ppermute | solution.py:290
  7.4 4.6 %collective-permute-start.1 = (bf16[1,8,1024]{2,1,0:T(8,128)(2,1)S(1)}, bf16[1,8,1024]{2,1,0:T(8,128)(2,1)S(1)}, u32[]{:S(2)}, u32[]{:S(2)}) collective-permute-start(bf16[1,8,1024]{2,1,0:T(8,128)(2,1)S(1)} %bitcast.8), channel_id=1, source_target_pairs={{0,12},{4,8},{8,0},{12,4},{1,13},{5,9},{9,1},{13,5},{2,14},{6,10},... | collective-permute-start | bytes 49160 | tf_op jit(solution)/shard_map/ppermute | solution.py:290
  8.5 3.7 %collective-permute-start = (bf16[1,8,1024]{2,1,0:T(8,128)(2,1)S(1)}, bf16[1,8,1024]{2,1,0:T(8,128)(2,1)S(1)}, u32[]{:S(2)}, u32[]{:S(2)}) collective-permute-start(bf16[1,8,1024]{2,1,0:T(8,128)(2,1)S(1)} %bitcast.9), channel_id=1, source_target_pairs={{0,4},{4,0},{8,12},{12,8},{1,5},{5,1},{9,13},{13,9},{2,6},{6,2},{1... | collective-permute-start | bytes 49160 | tf_op jit(solution)/shard_map/ppermute | solution.py:290
  13.0 1.4 %collective-permute-start.3 = (f32[200,128]{1,0:T(8,128)S(1)}, f32[200,128]{1,0:T(8,128)S(1)}, u32[]{:S(2)}, u32[]{:S(2)}) collective-permute-start(f32[200,128]{1,0:T(8,128)S(1)} %get-tuple-element.60), channel_id=1, source_target_pairs={{0,1},{1,0},{2,3},{3,2},{4,5},{5,4},{6,7},{7,6},{8,9},{9,8},{10,11... | collective-permute-start | bytes 307208 | tf_op jit(solution)/shard_map/ppermute | solution.py:274
  14.4 5.1 %collective-permute-start.6 = (bf16[200,128]{1,0:T(8,128)(2,1)S(1)}, bf16[200,128]{1,0:T(8,128)(2,1)S(1)}, u32[]{:S(2)}, u32[]{:S(2)}) collective-permute-start(bf16[200,128]{1,0:T(8,128)(2,1)S(1)} %add_convert_fusion.1), channel_id=1, source_target_pairs={{0,6},{1,7},{2,4},{3,5},{4,2},{5,3},{6,0},{7,1},{8,14},{9,15},{10,... | collective-permute-start | bytes 153608 | tf_op jit(solution)/shard_map/ppermute | solution.py:326
  16.8 4.0 %collective-permute-start.5 = (bf16[200,128]{1,0:T(8,128)(2,1)S(1)}, bf16[200,128]{1,0:T(8,128)(2,1)S(1)}, u32[]{:S(2)}, u32[]{:S(2)}) collective-permute-start(bf16[200,128]{1,0:T(8,128)(2,1)S(1)} %add_convert_fusion.1), channel_id=1, source_target_pairs={{0,5},{1,4},{2,7},{3,6},{4,1},{5,0},{6,3},{7,2},{8,12},{9,13},{10,... | collective-permute-start | bytes 153608 | tf_op jit(solution)/shard_map/ppermute | solution.py:326
  17.1 3.7 %collective-permute-start.4 = (bf16[200,128]{1,0:T(8,128)(2,1)S(1)}, bf16[200,128]{1,0:T(8,128)(2,1)S(1)}, u32[]{:S(2)}, u32[]{:S(2)}) collective-permute-start(bf16[200,128]{1,0:T(8,128)(2,1)S(1)} %add_convert_fusion.1), channel_id=1, source_target_pairs={{0,3},{1,2},{2,1},{3,0},{4,7},{5,6},{6,5},{7,4},{8,11},{9,10},{10,... | collective-permute-start | bytes 153608 | tf_op jit(solution)/shard_map/ppermute | solution.py:326
  20.9 4.5 %collective-permute-start.7 = (bf16[200,128]{1,0:T(8,128)(2,1)S(1)}, bf16[200,128]{1,0:T(8,128)(2,1)S(1)}, u32[]{:S(2)}, u32[]{:S(2)}) collective-permute-start(bf16[200,128]{1,0:T(8,128)(2,1)S(1)} %add_convert_fusion), channel_id=1, source_target_pairs={{0,9},{1,8},{2,11},{3,10},{4,14},{5,15},{6,13},{7,12},{8,1},{9,0},... | collective-permute-start | bytes 153608 | tf_op jit(solution)/shard_map/ppermute | solution.py:326
  25.4 1.5 %collective-permute-start.8 = (f32[200,128]{1,0:T(8,128)S(1)}, f32[200,128]{1,0:T(8,128)S(1)}, u32[]{:S(2)}, u32[]{:S(2)}) collective-permute-start(f32[200,128]{1,0:T(8,128)S(1)} %convert_add_fusion.total), channel_id=1, source_target_pairs={{0,1},{1,0},{2,3},{3,2},{4,5},{5,4},{6,7},{7,6},{8,9},{9,8},{10,11... | collective-permute-start | bytes 307208 | tf_op jit(solution)/shard_map/ppermute | solution.py:274

commit v7 on v5

--- a/solution.py
+++ b/solution.py
@@ -274,7 +274,7 @@
 
 def sum_parameters(keep, away, link_dtype):
     assert lax.axis_size("sample") == 2
-    sent = (keep + swap(away, 1)).astype(link_dtype)
+    sent = (keep + swap(away.astype(link_dtype), 1).astype(f32)).astype(link_dtype)
     tile_bits, member_bits = chip_bits()
     groups = rounds_of(tile_bits + member_bits)
     for place, group in enumerate(groups):

time: 27.7 us -> 27.7 us (level)
  no operation moved by 1% of the time
where the time goes in v7:
time: 27.7 us; the launch traced here: 27.5 us
  starting transfers between devices  11.4 us (41%)
  waiting for transfers between devices  9.57 us (35%)
  Pallas kernels  5.13 us (19%)
  between operations  1.34 us (5%)
    ppermute x4, waiting for transfers between devices, cross(): return lax.ppermute(array, mesh_axes, pairs)  5.75 us
    ppermute x3, starting transfers between devices, gather_members(): lax.ppermute(block[None], 'member', list(enumerate(route)))  5.67 us
    ppermute x4, starting transfers between devices, cross(): return lax.ppermute(array, mesh_axes, pairs)  5.16 us
    ppermute x3, waiting for transfers between devices, gather_members(): lax.ppermute(block[None], 'member', list(enumerate(route)))  2.29 us
    pallas_call x1, Pallas kernels, on_device(): pl.pallas_call(functools.partial(forward_kernel, chunk), grid=(steps,), i...  2.05 us
    ppermute x2, waiting for transfers between devices, swap(): lax.ppermute(array, mesh_axes, [(place, place ^ offset) for place in rang...  1.53 us
    pallas_call x1, Pallas kernels, on_device(): pl.pallas_call(derivative_kernel, grid=(steps,), in_specs=[by_point((poin...  0.94 us
    pallas_call x1, Pallas kernels, on_device(): pl.pallas_call(functools.partial(backward_kernel, steps, norm_factor / me...  0.75 us
  transfers between devices with their start and end apart: 9, of which 8 were waited for; matrix products, arithmetic and copies ran while one was open for 0% of the time, Pallas kernels for 6%

profile of v7, /device:TPU:0, one launch (start us, length us, event | category | flops | bytes accessed | tf_op | source)
XLA Modules:
  0.0 27.5 jit_solution(9505122267571921460)
XLA Ops:
  1.3 2.1 %forward.1 = (bf16[1024,256]{1,0:T(8,128)(2,1)S(1)}, f32[8,4,256]{2,1,0:T(4,128)S(1)}, s32[4,256]{1,0:T(4,128)S(1)}, f32[1024,128]{1,0:T(8,128)S(1)}, f32[1024,1...) custom-call(s32[1,1]{1,0:T(1,128)S(6)} %copy.13.order, ...), custom_call_target="tpu_custom_call" | custom-call | tf_op jit(solution)/shard_map/forward/pallas_call | solution.py:340
  3.3 4.1 %collective-permute-start.2 = (bf16[1,8,1024]{2,1,0:T(8,128)(2,1)S(1)}, bf16[1,8,1024]{2,1,0:T(8,128)(2,1)S(1)}, u32[]{:S(2)}, u32[]{:S(2)}) collective-permute-start(bf16[1,8,1024]{2,1,0:T(8,128)(2,1)S(1)} %bitcast.7), channel_id=1, source_target_pairs={{0,8},{4,12},{8,4},{12,0},{1,9},{5,13},{9,5},{13,1},{2,10},{6,14},... | collective-permute-start | bytes 49160 | tf_op jit(solution)/shard_map/ppermute | solution.py:236
  7.4 1.1 %collective-permute-start.1 = (bf16[1,8,1024]{2,1,0:T(8,128)(2,1)S(1)}, bf16[1,8,1024]{2,1,0:T(8,128)(2,1)S(1)}, u32[]{:S(2)}, u32[]{:S(2)}) collective-permute-start(bf16[1,8,1024]{2,1,0:T(8,128)(2,1)S(1)} %bitcast.8), channel_id=1, source_target_pairs={{0,12},{4,8},{8,0},{12,4},{1,13},{5,9},{9,1},{13,5},{2,14},{6,10},... | collective-permute-start | bytes 49160 | tf_op jit(solution)/shard_map/ppermute | solution.py:236
  8.5 0.5 %collective-permute-start = (bf16[1,8,1024]{2,1,0:T(8,128)(2,1)S(1)}, bf16[1,8,1024]{2,1,0:T(8,128)(2,1)S(1)}, u32[]{:S(2)}, u32[]{:S(2)}) collective-permute-start(bf16[1,8,1024]{2,1,0:T(8,128)(2,1)S(1)} %bitcast.9), channel_id=1, source_target_pairs={{0,4},{4,0},{8,12},{12,8},{1,5},{5,1},{9,13},{13,9},{2,6},{6,2},{1... | collective-permute-start | bytes 49160 | tf_op jit(solution)/shard_map/ppermute | solution.py:236
  9.0 0.9 %derivatives.1 = (f32[1024,128]{1,0:T(8,128)S(1)}, f32[1024,128]{1,0:T(8,128)S(1)}, f32[1024,128]{1,0:T(8,128)S(1)}, bf16[256,1024]{1,0:T(8,128)(2,1)S(1)}, bf16...) custom-call(bf16[1024,256]{1,0:T(8,128)(2,1)S(1)} %get-tuple-element.33.latent, ...), custom_call_target="tpu_custom_call" | custom-call | tf_op jit(solution)/shard_map/derivatives/pallas_call | solution.py:366
  10.0 0.2 collective-permute-done.2.refs_2_.refs_5_
  10.2 1.9 %collective-permute-done.1.refs_1_.refs_4_ = bf16[1,8,1024]{2,1,0:T(8,128)(2,1)S(1)} collective-permute-done((bf16[1,8,1024]{2,1,0:T(8,128)(2,1)S(1)}, bf16[1,8,1024]{2,1,0:T(8,128)(2,1)S(1)}, u32[]{:S(2)}, u32[]{:S(2)}) %collective-permute-start.1) | collective-permute-done | bytes 16416 | tf_op jit(solution)/shard_map/ppermute | solution.py:236
  12.1 0.2 collective-permute-done.refs_0_.refs_3_
  12.2 0.7 %backward.1 = (f32[200,128]{1,0:T(8,128)S(1)}, f32[200,128]{1,0:T(8,128)S(1)}) custom-call(s32[1,1]{1,0:T(1,128)S(6)} %copy.13.order, f32[8,1024]{1,0:T(8,128)S(1)} %get-tuple-element.32.predicted.refs_0_, f32[8,1024]{1,0:T(8,128)S(1)} %get-tuple-element.42.target.refs_1_, f32[1,1024]{1,0:T(1,128)S(1)} %get-tuple-element.43.valid.refs_2_, ...), custom_call_target="tpu_custom_call" | custom-call | tf_op jit(solution)/shard_map/backward/pallas_call | solution.py:380
  13.0 0.1 collective-permute-start.3
  13.1 1.2 %collective-permute-done.3 = bf16[200,128]{1,0:T(8,128)(2,1)S(1)} collective-permute-done((bf16[200,128]{1,0:T(8,128)(2,1)S(1)}, bf16[200,128]{1,0:T(8,128)(2,1)S(1)}, u32[]{:S(2)}, u32[]{:S(2)}) %collective-permute-start.3) | collective-permute-done | bytes 51232 | tf_op jit(solution)/shard_map/ppermute | solution.py:220
  14.3 2.4 %collective-permute-start.6 = (bf16[200,128]{1,0:T(8,128)(2,1)S(1)}, bf16[200,128]{1,0:T(8,128)(2,1)S(1)}, u32[]{:S(2)}, u32[]{:S(2)}) collective-permute-start(bf16[200,128]{1,0:T(8,128)(2,1)S(1)} %add_convert_fusion.1), channel_id=1, source_target_pairs={{0,6},{1,7},{2,4},{3,5},{4,2},{5,3},{6,0},{7,1},{8,14},{9,15},{10,... | collective-permute-start | bytes 153608 | tf_op jit(solution)/shard_map/ppermute | solution.py:272
  16.7 0.3 collective-permute-start.5
  17.0 0.6 %collective-permute-start.4 = (bf16[200,128]{1,0:T(8,128)(2,1)S(1)}, bf16[200,128]{1,0:T(8,128)(2,1)S(1)}, u32[]{:S(2)}, u32[]{:S(2)}) collective-permute-start(bf16[200,128]{1,0:T(8,128)(2,1)S(1)} %add_convert_fusion.1), channel_id=1, source_target_pairs={{0,3},{1,2},{2,1},{3,0},{4,7},{5,6},{6,5},{7,4},{8,11},{9,10},{10,... | collective-permute-start | bytes 153608 | tf_op jit(solution)/shard_map/ppermute | solution.py:272
  17.6 1.8 %collective-permute-done.6 = bf16[200,128]{1,0:T(8,128)(2,1)S(1)} collective-permute-done((bf16[200,128]{1,0:T(8,128)(2,1)S(1)}, bf16[200,128]{1,0:T(8,128)(2,1)S(1)}, u32[]{:S(2)}, u32[]{:S(2)}) %collective-permute-start.6) | collective-permute-done | bytes 51232 | tf_op jit(solution)/shard_map/ppermute | solution.py:272
  19.4 1.3 %collective-permute-done.5 = bf16[200,128]{1,0:T(8,128)(2,1)S(1)} collective-permute-done((bf16[200,128]{1,0:T(8,128)(2,1)S(1)}, bf16[200,128]{1,0:T(8,128)(2,1)S(1)}, u32[]{:S(2)}, u32[]{:S(2)}) %collective-permute-start.5) | collective-permute-done | bytes 51232 | tf_op jit(solution)/shard_map/ppermute | solution.py:272
  20.8 0.0 collective-permute-done.4
  20.8 1.9 %collective-permute-start.7 = (bf16[200,128]{1,0:T(8,128)(2,1)S(1)}, bf16[200,128]{1,0:T(8,128)(2,1)S(1)}, u32[]{:S(2)}, u32[]{:S(2)}) collective-permute-start(bf16[200,128]{1,0:T(8,128)(2,1)S(1)} %add_convert_fusion), channel_id=1, source_target_pairs={{0,9},{1,8},{2,11},{3,10},{4,14},{5,15},{6,13},{7,12},{8,1},{9,0},... | collective-permute-start | bytes 153608 | tf_op jit(solution)/shard_map/ppermute | solution.py:272
  22.7 2.6 %collective-permute-done.7 = bf16[200,128]{1,0:T(8,128)(2,1)S(1)} collective-permute-done((bf16[200,128]{1,0:T(8,128)(2,1)S(1)}, bf16[200,128]{1,0:T(8,128)(2,1)S(1)}, u32[]{:S(2)}, u32[]{:S(2)}) %collective-permute-start.7) | collective-permute-done | bytes 51232 | tf_op jit(solution)/shard_map/ppermute | solution.py:272
  25.3 0.5 %collective-permute-start.8 = (f32[200,128]{1,0:T(8,128)S(1)}, f32[200,128]{1,0:T(8,128)S(1)}, u32[]{:S(2)}, u32[]{:S(2)}) collective-permute-start(f32[200,128]{1,0:T(8,128)S(1)} %convert_add_fusion.total), channel_id=1, source_target_pairs={{0,1},{1,0},{2,3},{3,2},{4,5},{5,4},{6,7},{7,6},{8,9},{9,8},{10,11... | collective-permute-start | bytes 307208 | tf_op jit(solution)/shard_map/ppermute | solution.py:220
  25.8 0.6 %score.1 = f32[8,1,256]{2,1,0:T(1,128)} custom-call(f32[8,1024]{1,0:T(8,128)S(1)} %get-tuple-element.32.predicted.refs_0_, f32[8,1024]{1,0:T(8,128)S(1)} %get-tuple-element.42.target.refs_1_, f32[1,1024]{1,0:T(1,128)S(1)} %get-tuple-element.43.valid.refs_2_, bf16[1,8,1024]{2,1,0:T(8,128)(2,1)S(1)} %collective-permute-done.refs_0_.refs_3_, ...), custom_call_target="tpu_custom_call" | custom-call | tf_op jit(solution)/shard_map/score/pallas_call | solution.py:406
  26.5 0.3 %collective-permute-done.8.other = f32[200,128]{1,0:T(8,128)S(1)} collective-permute-done((f32[200,128]{1,0:T(8,128)S(1)}, f32[200,128]{1,0:T(8,128)S(1)}, u32[]{:S(2)}, u32[]{:S(2)}) %collective-permute-start.8) | collective-permute-done | bytes 102432 | tf_op jit(solution)/shard_map/ppermute | solution.py:220
  26.8 0.7 %gradients.1 = (f32[256,128]{1,0:T(8,128)}, f32[128,128]{1,0:T(8,128)}, f32[8,128]{1,0:T(8,128)}, f32[4,128]{1,0:T(4,128)}) custom-call(f32[200,128]{1,0:T(8,128)S(1)} %convert_add_fusion.total, f32[200,128]{1,0:T(8,128)S(1)} %collective-permute-done.8.other), custom_call_target="tpu_custom_call" | custom-call | tf_op jit(solution)/shard_map/gradients/pallas_call | solution.py:418
  (4 shorter events, 0.1 us)
Async XLA Ops:
  3.3 6.8 %collective-permute-start.2 = (bf16[1,8,1024]{2,1,0:T(8,128)(2,1)S(1)}, bf16[1,8,1024]{2,1,0:T(8,128)(2,1)S(1)}, u32[]{:S(2)}, u32[]{:S(2)}) collective-permute-start(bf16[1,8,1024]{2,1,0:T(8,128)(2,1)S(1)} %bitcast.7), channel_id=1, source_target_pairs={{0,8},{4,12},{8,4},{12,0},{1,9},{5,13},{9,5},{13,1},{2,10},{6,14},... | collective-permute-start | bytes 49160 | tf_op jit(solution)/shard_map/ppermute | solution.py:236
  7.4 4.6 %collective-permute-start.1 = (bf16[1,8,1024]{2,1,0:T(8,128)(2,1)S(1)}, bf16[1,8,1024]{2,1,0:T(8,128)(2,1)S(1)}, u32[]{:S(2)}, u32[]{:S(2)}) collective-permute-start(bf16[1,8,1024]{2,1,0:T(8,128)(2,1)S(1)} %bitcast.8), channel_id=1, source_target_pairs={{0,12},{4,8},{8,0},{12,4},{1,13},{5,9},{9,1},{13,5},{2,14},{6,10},... | collective-permute-start | bytes 49160 | tf_op jit(solution)/shard_map/ppermute | solution.py:236
  8.5 3.7 %collective-permute-start = (bf16[1,8,1024]{2,1,0:T(8,128)(2,1)S(1)}, bf16[1,8,1024]{2,1,0:T(8,128)(2,1)S(1)}, u32[]{:S(2)}, u32[]{:S(2)}) collective-permute-start(bf16[1,8,1024]{2,1,0:T(8,128)(2,1)S(1)} %bitcast.9), channel_id=1, source_target_pairs={{0,4},{4,0},{8,12},{12,8},{1,5},{5,1},{9,13},{13,9},{2,6},{6,2},{1... | collective-permute-start | bytes 49160 | tf_op jit(solution)/shard_map/ppermute | solution.py:236
  13.0 1.3 %collective-permute-start.3 = (bf16[200,128]{1,0:T(8,128)(2,1)S(1)}, bf16[200,128]{1,0:T(8,128)(2,1)S(1)}, u32[]{:S(2)}, u32[]{:S(2)}) collective-permute-start(bf16[200,128]{1,0:T(8,128)(2,1)S(1)} %convert_element_type.30), channel_id=1, source_target_pairs={{0,1},{1,0},{2,3},{3,2},{4,5},{5,4},{6,7},{7,6},{8,9},{9,8},{10,11... | collective-permute-start | bytes 153608 | tf_op jit(solution)/shard_map/ppermute | solution.py:220
  14.3 5.1 %collective-permute-start.6 = (bf16[200,128]{1,0:T(8,128)(2,1)S(1)}, bf16[200,128]{1,0:T(8,128)(2,1)S(1)}, u32[]{:S(2)}, u32[]{:S(2)}) collective-permute-start(bf16[200,128]{1,0:T(8,128)(2,1)S(1)} %add_convert_fusion.1), channel_id=1, source_target_pairs={{0,6},{1,7},{2,4},{3,5},{4,2},{5,3},{6,0},{7,1},{8,14},{9,15},{10,... | collective-permute-start | bytes 153608 | tf_op jit(solution)/shard_map/ppermute | solution.py:272
  16.7 4.0 %collective-permute-start.5 = (bf16[200,128]{1,0:T(8,128)(2,1)S(1)}, bf16[200,128]{1,0:T(8,128)(2,1)S(1)}, u32[]{:S(2)}, u32[]{:S(2)}) collective-permute-start(bf16[200,128]{1,0:T(8,128)(2,1)S(1)} %add_convert_fusion.1), channel_id=1, source_target_pairs={{0,5},{1,4},{2,7},{3,6},{4,1},{5,0},{6,3},{7,2},{8,12},{9,13},{10,... | collective-permute-start | bytes 153608 | tf_op jit(solution)/shard_map/ppermute | solution.py:272
  17.0 3.8 %collective-permute-start.4 = (bf16[200,128]{1,0:T(8,128)(2,1)S(1)}, bf16[200,128]{1,0:T(8,128)(2,1)S(1)}, u32[]{:S(2)}, u32[]{:S(2)}) collective-permute-start(bf16[200,128]{1,0:T(8,128)(2,1)S(1)} %add_convert_fusion.1), channel_id=1, source_target_pairs={{0,3},{1,2},{2,1},{3,0},{4,7},{5,6},{6,5},{7,4},{8,11},{9,10},{10,... | collective-permute-start | bytes 153608 | tf_op jit(solution)/shard_map/ppermute | solution.py:272
  20.8 4.5 %collective-permute-start.7 = (bf16[200,128]{1,0:T(8,128)(2,1)S(1)}, bf16[200,128]{1,0:T(8,128)(2,1)S(1)}, u32[]{:S(2)}, u32[]{:S(2)}) collective-permute-start(bf16[200,128]{1,0:T(8,128)(2,1)S(1)} %add_convert_fusion), channel_id=1, source_target_pairs={{0,9},{1,8},{2,11},{3,10},{4,14},{5,15},{6,13},{7,12},{8,1},{9,0},... | collective-permute-start | bytes 153608 | tf_op jit(solution)/shard_map/ppermute | solution.py:272
  25.3 1.4 %collective-permute-start.8 = (f32[200,128]{1,0:T(8,128)S(1)}, f32[200,128]{1,0:T(8,128)S(1)}, u32[]{:S(2)}, u32[]{:S(2)}) collective-permute-start(f32[200,128]{1,0:T(8,128)S(1)} %convert_add_fusion.total), channel_id=1, source_target_pairs={{0,1},{1,0},{2,3},{3,2},{4,5},{5,4},{6,7},{7,6},{8,9},{9,8},{10,11... | collective-permute-start | bytes 307208 | tf_op jit(solution)/shard_map/ppermute | solution.py:220
